TPU v7x, 256 devices: a whole 4x4x8 slice. The times are simulated.
256 devices in a mesh: dp: 8 (over y, core), ctx: 32 (over z, x).
Axes of the slice: x: 4, y: 4, z: 8, core: 2. Of those that a mesh axis runs over, the one named last changes fastest.
Arguments:
- text_rows: bfloat16 [8, 4096, 5120], P('dp', 'ctx'), may hold values from -5 to 5
- image_rows: bfloat16 [8, 256, 5120], P('dp', 'ctx'), may hold values from -5 to 5
- tile_counts: int32 [8, 32], P('dp', 'ctx'), may hold values from 1 to 8, as said below
- tile_offsets: int32 [8, 32], P('dp', 'ctx'), may hold values from 0 to 4088, as said below
- doc_ids: int32 [8, 4096], P('dp', 'ctx'), may hold values from 0 to 7, never falling along the last dimension, each value on 1 to 2176 neighbouring positions
- out_grad: bfloat16 [8, 4096, 4096], P('dp', 'ctx'), may hold values from -6 to 6
- proj_scale: float32 [5120], replicated, may hold values from 0.5 to 1.5
- proj_shift: float32 [5120], replicated, may hold values from -3 to 3
Outputs:
- attn_out: bfloat16 [8, 4096, 4096], P('dp', 'ctx')
- text_grad: bfloat16 [8, 4096, 5120], P('dp', 'ctx')
- image_grad: bfloat16 [8, 256, 5120], P('dp', 'ctx')
- scale_grad: float32 [5120], replicated
- shift_grad: float32 [5120], replicated
Inputs may be any that keep to these rules, and one draw needn't show every extreme that they name: `tile_counts`: in every sequence one owner's count is exactly 8. The images of one sequence do not intersect and end within the sequence: tile_offsets + tile_counts <= 4096; in every sequence one image ends exactly at position 4096.
All inputs are finite; a program needn't handle non-finite values.
Results may differ from a plain program's by a relative error of at most 0.02.
Values may be sent and summed in bfloat16 or wider, within the bound.
A program may use at most 64 MiB of HBM per device.

v0:
```python
from functools import partial

import jax
import jax.numpy as jnp
from jax import lax
from jax.sharding import PartitionSpec as P

HD = 128
HEADS = 32
KVH = 4
DOCS = 8


def per_device(
    text_rows, image_rows, tile_counts, tile_offsets, doc_ids, out_grad, proj_scale, proj_shift
):
    n_ctx = lax.axis_size("ctx")
    my_index = lax.axis_index("ctx")
    tok_rows = text_rows.shape[1]
    slots = image_rows.shape[1]
    rep = HEADS // KVH
    qwidth = HEADS * HD
    half_kv = KVH * HD
    score_scale = HD ** (-0.5)
    base = my_index * tok_rows
    docs = doc_ids[0]
    owners = jnp.arange(n_ctx, dtype=jnp.int32)
    match = docs[:, None] == jnp.arange(DOCS, dtype=jnp.int32)[None, :]
    histogram = jnp.sum(match.astype(jnp.int32), axis=0)
    own_entry = jnp.stack([tile_counts[0, 0], tile_offsets[0, 0]])
    table = jnp.where((owners == my_index)[:, None], own_entry[None, :], 0)
    totals, layout = lax.psum((histogram, table), "ctx")
    counts_all = layout[:, 0]
    offsets_all = layout[:, 1]
    before = jnp.cumsum(totals) - totals
    doc_start = jnp.sum(jnp.where(match, before[None, :], 0), axis=1)
    positions = base + jnp.arange(tok_rows, dtype=jnp.int32)
    covered = (positions[:, None] >= offsets_all[None, :]) & (
        positions[:, None] < (offsets_all + counts_all)[None, :]
    )
    is_image = jnp.any(covered, axis=1)
    owner_of = jnp.sum(jnp.where(covered, owners[None, :], 0), axis=1)
    first_of = jnp.sum(jnp.where(covered, offsets_all[None, :], 0), axis=1)
    slot_of = jnp.where(is_image, owner_of * slots + positions - first_of, 0)
    adapted = (image_rows[0].astype(jnp.float32) * proj_scale + proj_shift).astype(jnp.bfloat16)
    every_image = lax.all_gather(adapted, "ctx", axis=0, tiled=True)
    picked = jnp.take(every_image, slot_of, axis=0)
    rows = jnp.where(is_image[:, None], picked, text_rows[0])
    query = rows[:, :qwidth].reshape(tok_rows, KVH, rep, HD)
    keyval = rows[:, qwidth:]
    dout = out_grad[0].reshape(tok_rows, KVH, rep, HD)
    first_key = doc_start[0]
    last_pos = base + tok_rows - 1

    def block_terms(block, kstart):
        count = block.shape[0]
        keys = block[:, :half_kv].reshape(count, KVH, HD)
        vals = block[:, half_kv:].reshape(count, KVH, HD)
        key_pos = kstart + jnp.arange(count, dtype=jnp.int32)
        allowed = (key_pos[None, :] <= positions[:, None]) & (
            key_pos[None, :] >= doc_start[:, None]
        )
        scores = (
            jnp.einsum("pgrd,tgd->grpt", query, keys, preferred_element_type=jnp.float32)
            * score_scale
        )
        return (keys, vals, allowed[None, None], scores)

    def sweep(carry, piece, step):
        piece_rows = piece.shape[0]
        block_rows = 512

        def visit(index, state):
            kstart = index * block_rows
            block = lax.dynamic_slice_in_dim(piece, index * block_rows, block_rows, 0)
            active = (kstart <= last_pos) & (kstart + block_rows - 1 >= first_key)
            return lax.cond(
                active, lambda inner: step(inner, block, kstart), lambda inner: inner, state
            )

        return lax.fori_loop(0, piece_rows // block_rows, visit, carry)

    def forward_step(state, block, kstart):
        row_max, row_total, weighted = state
        keys, vals, allowed, scores = block_terms(block, kstart)
        new_max = jnp.maximum(row_max, jnp.max(jnp.where(allowed, scores, -1e30), axis=-1))
        factor = jnp.exp(row_max - new_max)
        expd = jnp.where(allowed, jnp.exp(scores - new_max[..., None]), 0.0)
        row_total = row_total * factor + jnp.sum(expd, axis=-1)
        weighted = weighted * factor[..., None] + jnp.einsum(
            "grpt,tgd->grpd", expd.astype(jnp.bfloat16), vals, preferred_element_type=jnp.float32
        )
        return (new_max, row_total, weighted)

    def backward_step(anchor, state, block, kstart):
        query_acc, keyval_grad = state
        count = block.shape[0]
        keys, vals, allowed, scores = block_terms(block, kstart)
        prob = jnp.where(allowed, jnp.exp(scores - log_total[..., None]), 0.0)
        prob_b = prob.astype(jnp.bfloat16)
        dprob = jnp.einsum("pgrd,tgd->grpt", dout, vals, preferred_element_type=jnp.float32)
        dscore = (prob * (dprob - corr[..., None]) * score_scale).astype(jnp.bfloat16)
        query_acc = query_acc + jnp.einsum(
            "grpt,tgd->grpd", dscore, keys, preferred_element_type=jnp.float32
        )
        key_part = jnp.einsum("grpt,pgrd->tgd", dscore, query, preferred_element_type=jnp.float32)
        val_part = jnp.einsum("grpt,pgrd->tgd", prob_b, dout, preferred_element_type=jnp.float32)
        piece_grad = jnp.concatenate(
            [key_part.reshape(count, half_kv), val_part.reshape(count, half_kv)], axis=1
        )
        keyval_grad = lax.dynamic_update_slice_in_dim(keyval_grad, piece_grad, kstart - anchor, 0)
        return (query_acc, keyval_grad)

    forward_init = (
        jnp.full((KVH, rep, tok_rows), -1e30, jnp.float32),
        jnp.zeros((KVH, rep, tok_rows), jnp.float32),
        jnp.zeros((KVH, rep, tok_rows, HD), jnp.float32),
    )
    query_init = jnp.zeros((KVH, rep, tok_rows, HD), jnp.float32)
    row_max, row_total, weighted = sweep(
        forward_init, lax.all_gather(keyval, "ctx", axis=0, tiled=True), forward_step
    )
    attn = (weighted / row_total[..., None]).astype(jnp.bfloat16)
    log_total = row_max + jnp.log(row_total)
    corr = jnp.einsum("pgrd,grpd->grp", dout, attn, preferred_element_type=jnp.float32)
    attn_out = attn.transpose(2, 0, 1, 3).reshape(1, tok_rows, qwidth)
    backward_init = (query_init, jnp.zeros((n_ctx * tok_rows, 2 * half_kv), jnp.float32))
    query_acc, keyval_grad = sweep(
        backward_init, lax.all_gather(keyval, "ctx", axis=0, tiled=True), partial(backward_step, 0)
    )
    keyval_own = lax.psum_scatter(
        keyval_grad.astype(jnp.bfloat16), "ctx", scatter_dimension=0, tiled=True
    )
    query_grad = query_acc.astype(jnp.bfloat16).transpose(2, 0, 1, 3).reshape(tok_rows, qwidth)
    grad_rows = jnp.concatenate([query_grad, keyval_own], axis=1)
    text_grad = jnp.where(is_image[:, None], jnp.zeros((), jnp.bfloat16), grad_rows)[None]
    selector = is_image[:, None] & (
        slot_of[:, None] == jnp.arange(n_ctx * slots, dtype=jnp.int32)[None, :]
    )
    selector = selector.astype(jnp.bfloat16)
    scattered = jnp.dot(selector.T, grad_rows, preferred_element_type=jnp.float32)
    adapted_grad = lax.psum_scatter(
        scattered.astype(jnp.bfloat16), "ctx", scatter_dimension=0, tiled=True
    )
    grad_f = adapted_grad.astype(jnp.float32)
    image_grad = (grad_f * proj_scale).astype(jnp.bfloat16)[None]
    scale_part = jnp.sum(grad_f * image_rows[0].astype(jnp.float32), axis=0)
    shift_part = jnp.sum(grad_f, axis=0)
    scale_grad, shift_grad = lax.psum((scale_part, shift_part), ("dp", "ctx"))
    return (attn_out, text_grad, image_grad, scale_grad, shift_grad)


def solution(mesh):
    return jax.shard_map(
        per_device,
        mesh=mesh,
        in_specs=(
            P("dp", "ctx", None),
            P("dp", "ctx", None),
            P("dp", "ctx"),
            P("dp", "ctx"),
            P("dp", "ctx"),
            P("dp", "ctx", None),
            P(),
            P(),
        ),
        out_specs=(P("dp", "ctx", None), P("dp", "ctx", None), P("dp", "ctx", None), P(), P()),
        check_vma=False,
    )
```

profile of v0, /device:TPU:8, one launch (start us, length us, event | category | flops | bytes accessed | tf_op | source)
XLA Modules:
  0.0 890.6 jit_solution(6951090291228874337)
XLA Ops:
  11.1 23.4 %all-reduce = (s32[8]{0:T(128)S(1)}, s32[32,2]{0,1:T(2,128)S(1)}) all-reduce(s32[8]{0:T(128)S(1)} %convert_reduce_fusion.1, s32[32,2]{0,1:T(2,128)S(1)} %broadcast_select_fusion), channel_id=1, replica_groups=mesh['dp'=8,'ctx'=32] {'ctx'}, use_global_device_ids=true, to_apply=%region_5.6 | all-reduce | flops 72 | bytes 576 | tf_op jit(solution)/shard_map/psum | solution.py:32
  35.2 57.7 %all-gather.3.cloned.1.call-done = bf16[256,5120]{1,0:T(8,128)(2,1)} async-done(((bf16[8,5120]{1,0:T(8,128)(2,1)}), bf16[256,5120]{1,0:T(8,128)(2,1)}) %all-gather.3.cloned.1.call-update) | async-done | bytes 2621456 | tf_op jit(solution)/shard_map/all_gather | solution.py:46
  92.9 4.7 gather_fusion
  97.7 1.7 bitcast_select_fusion.1
  106.0 90.6 %all-gather.5.cloned.1.call-done = bf16[4096,1024]{1,0:T(8,128)(2,1)} async-done(((bf16[128,1024]{1,0:T(8,128)(2,1)}), bf16[4096,1024]{1,0:T(8,128)(2,1)}) %all-gather.5.cloned.1.call-update) | async-done | bytes 8388624 | tf_op jit(solution)/shard_map/all_gather | solution.py:121
  196.6 11.3 %copy.76 = bf16[4096,1024]{0,1:T(8,128)(2,1)} copy(bf16[4096,1024]{1,0:T(8,128)(2,1)} %all-gather.5.cloned.1.call-done) | data formatting | bytes 16777216
  209.5 10.0 %while.42 = (s32[]{:T(128)}, f32[4,8,128]{2,1,0:T(8,128)S(1)}, f32[4,8,128]{2,1,0:T(8,128)S(1)}, f32[4,8,128,128]{3,2,1,0:T(8,128)}, s32[]{:T(128)}, /*index=5*/...) while((s32[]{:T(128)}, f32[4,8,128]{2,1,0:T(8,128)S(1)}, ...), condition=%wide.region_13.14_spmd.clone, body=%wide.region_8.13_spmd.clone.sunk | while | flops 1098064512 | bytes 50863008 | solution.py:81
  209.6 9.2 %conditional.6 = ((f32[4,8,128]{2,1,0:T(8,128)S(1)}, f32[4,8,128]{2,1,0:T(8,128)S(1)}, f32[4,8,128,128]{3,2,1,0:T(8,128)})) conditional(s32[]{:T(128)} %convert_element_type.115, (f32[4,8,128]{2,1,0:T(8,128)S(1)}, f32[4,8,128]{2,1,0:T(8,128)S(1)}, f32[4,8,128,128]{3,2,1,0:T(8,128)}) %tuple.153, (s32[]{:T(128)}, s32[]{:T(128)}, s32[128]{0:T(128)S(1)}, ...), branch_computations={%region_9.9_spmd, %region_10.12_spmd} | conditional | flops 1098064512 | bytes 50862228 | solution.py:77
  212.5 1.8 fusion.8
  214.3 3.1 multiply_add_fusion
  219.5 2.7 fusion.46
  222.2 1.9 copy.102
  224.1 2.2 multiply_reduce_fusion
  226.5 4.3 broadcast_in_dim.182
  230.8 13.4 %while.43 = (s32[]{:T(128)}, f32[4,8,128,128]{3,2,1,0:T(8,128)S(1)}, bf16[4096,1024]{0,1:T(8,128)(2,1)}, s32[]{:T(128)}, s32[]{:T(128)S(1)}, /*index=5*/s32[128]...) while((s32[]{:T(128)}, ...), condition=%wide.region_17.18_spmd.clone, body=%wide.region_14.17_spmd.clone.sunk | while | flops 2710241792 | bytes 57400216 | solution.py:81
  230.8 12.7 %conditional.7 = ((f32[4,8,128,128]{3,2,1,0:T(8,128)S(1)}, bf16[4096,1024]{0,1:T(8,128)(2,1)})) conditional(s32[]{:T(128)} %convert_element_type.116, (f32[4,8,128,128]{3,2,1,0:T(8,128)S(1)}, bf16[4096,1024]{0,1:T(8,128)(2,1)}) %tuple.156, (s32[]{:T(128)}, s32[]{:T(128)}, s32[128]{0:T(128)S(1)}, bf16[4096,1024]{0,1:T(8,128)(2,1)}, ...), branch_computations={%region_15.15_spmd, %region_16.16_spmd} | conditional | flops 2710241792 | bytes 57399412 | solution.py:77
  233.6 1.8 fusion.25
  235.4 3.1 fusion.21
  240.0 2.4 convolution_add_fusion
  244.2 12.0 %copy.114 = bf16[4096,1024]{1,0:T(8,128)(2,1)} copy(bf16[4096,1024]{0,1:T(8,128)(2,1)} %get-tuple-element.925) | data formatting | bytes 16777216
  257.0 331.7 %reduce-scatter.7.cloned.1.call-done = bf16[128,1024]{1,0:T(8,128)(2,1)} async-done(((bf16[4096,1024]{1,0:T(8,128)(2,1)}), bf16[128,1024]{1,0:T(8,128)(2,1)}) %reduce-scatter.7.cloned.1.call-update) | async-done | bytes 262160
  589.8 2.5 convolution_convert_fusion
  596.4 212.1 %reduce-scatter.5.cloned.1.call-done = bf16[8,5120]{1,0:T(8,128)(2,1)} async-done(((bf16[256,5120]{1,0:T(8,128)(2,1)}), bf16[8,5120]{1,0:T(8,128)(2,1)}) %reduce-scatter.5.cloned.1.call-update) | async-done | bytes 81936 | tf_op jit(solution)/shard_map/reduce_scatter | solution.py:142
  810.0 74.0 %all-reduce.1 = (f32[5120]{0:T(1024)}, f32[5120]{0:T(1024)}) all-reduce(f32[5120]{0:T(1024)S(1)} %get-tuple-element.1076, f32[5120]{0:T(1024)S(1)} %get-tuple-element.1075), channel_id=1, replica_groups=mesh['dp'=8,'ctx'=32] {'dp','ctx'}, use_global_device_ids=true, to_apply=%region_21.22 | all-reduce | flops 10240 | bytes 81920 | tf_op jit(solution)/shard_map/psum | solution.py:149
  (112 shorter events, 29.2 us)
Async XLA Ops:
  7.2 85.8 %all-gather.3.cloned.1.call-start = ((), (), s32[]{:S(2)}) async-start(), calls=%async_computation.2 | async-start | bytes 2703360 | tf_op jit(solution)/shard_map/all_gather | solution.py:46
  8.8 187.8 %all-gather.5.cloned.1.call-start = ((), (), s32[]{:S(2)}) async-start(), calls=%async_computation.3 | async-start | bytes 8650752 | tf_op jit(solution)/shard_map/all_gather | solution.py:121
  34.6 63.1 %copy-start.8 = (pred[128]{0:T(512)(128)(4,1)}, pred[128]{0:T(512)(128)(4,1)S(1)}, u32[]{:S(2)}) copy-start(pred[128]{0:T(512)(128)(4,1)S(1)} %fusion.43) | copy-start | bytes 388
  97.6 4.0 copy-start.5
  97.6 5.3 copy-start.11
  99.4 1.1 copy-start.2
  101.2 487.5 %reduce-scatter.7.cloned.1.call-start = ((), (), s32[]{:S(2)}) async-start(), calls=%async_computation.5 | async-start | bytes 8650752
  212.5 1.8 copy-start
  217.4 1.4 copy-start.1
  232.3 1.3 copy-start.3
  256.2 333.7 %copy-start.9 = (pred[128]{0:T(512)(128)(4,1)S(1)}, pred[128]{0:T(512)(128)(4,1)}, u32[]{:S(2)}) copy-start(pred[128]{0:T(512)(128)(4,1)} %copy-done.8) | copy-start | bytes 388
  256.2 333.7 %copy-start.10 = (s32[128]{0:T(128)S(1)}, s32[128]{0:T(128)}, u32[]{:S(2)}) copy-start(s32[128]{0:T(128)} %get-tuple-element.1130) | copy-start | bytes 1540
  256.2 552.3 %reduce-scatter.5.cloned.1.call-start = ((), (), s32[]{:S(2)}) async-start(), calls=%async_computation.4 | async-start | bytes 2703360 | tf_op jit(solution)/shard_map/reduce_scatter | solution.py:142
  257.0 335.4 %copy-start.4 = (bf16[128,4,8,128]{3,0,2,1:T(8,128)(2,1)S(1)}, bf16[128,4,8,128]{3,0,2,1:T(8,128)(2,1)}, u32[]{:S(2)}) copy-start(bf16[128,4,8,128]{3,0,2,1:T(8,128)(2,1)} %get-tuple-element.1138) | copy-start | bytes 3145732
  593.0 215.4 %copy-start.6 = (bf16[1,8,5120]{2,1,0:T(8,128)(2,1)S(1)}, bf16[1,8,5120]{2,1,0:T(8,128)(2,1)}, u32[]{:S(2)}) copy-start(bf16[1,8,5120]{2,1,0:T(8,128)(2,1)} %param.17) | copy-start | bytes 245764
  593.0 215.4 %copy-start.7 = (f32[5120]{0:T(1024)S(1)}, f32[5120]{0:T(1024)}, u32[]{:S(2)}) copy-start(f32[5120]{0:T(1024)} %param.22) | copy-start | bytes 61444
Sparse Core Ops, SparseCore 0:
  11.2 81.7 all-gather.2
  101.3 95.2 all-gather.4
  256.3 332.3 reduce-scatter.6
  592.9 215.5 reduce-scatter.4
where the time goes:
time: 893 us; the launch traced here: 891 us
  waiting for transfers between devices  692 us (77%)
  blocking collectives  97.4 us (11%)
  local copies, waits for them, and re-layouts  50.5 us (6%)
  matrix products  17 us (2%)
  other arithmetic  16.3 us (2%)
  between operations  15.3 us (2%)
    unnamed x5, waiting for transfers between devices  332 us
    reduce_scatter x1, waiting for transfers between devices, per_device(): lax.psum_scatter(scattered.astype(jnp.bfloat16), 'ctx', scatter_dimension...  212 us
    all_gather x1, waiting for transfers between devices, per_device(): lax.all_gather(keyval, 'ctx', axis=0, tiled=True)  90.6 us
    psum x1, blocking collectives, per_device(): scale_grad, shift_grad = lax.psum((scale_part, shift_part), ('dp', 'ctx'))  74 us
    all_gather x1, waiting for transfers between devices, per_device(): every_image = lax.all_gather(adapted, 'ctx', axis=0, tiled=True)  57.7 us
    unnamed x27, local copies, waits for them, and re-layouts  31.6 us
    psum x1, blocking collectives, per_device(): totals, layout = lax.psum((histogram, table), 'ctx')  23.4 us
  transfers between devices with their start and end apart: 4, of which 4 were waited for; matrix products, arithmetic and copies ran while one was open for 1% of the time, Pallas kernels for 0%

commit v1 on v0

v1 whole, which is shorter than its diff:
```python
import math

import jax
import jax.numpy as jnp
from jax import lax
from jax.experimental import pallas as pl
from jax.experimental.pallas import tpu as pltpu
from jax.sharding import PartitionSpec as P

MESH = pl.DeviceIdType.MESH
HD = 128
REP = 8
DOCS = 8
NZ = 8
NX = 4
NDP = 8
TOK = 128
ROW = NX * TOK
SLOTS = 8
NSLOT = NZ * NX * SLOTS
QC = REP * HD
HC = QC + 2 * HD
WIN = 6
HALF = HC // 2
SCALE = HD ** -0.5
LOG2E = math.log2(math.e)
F32 = jnp.float32
BF16 = jnp.bfloat16
NT = (((1,), (1,)), ((), ()))


def place():
    ctx = lax.axis_index("ctx")
    return lax.axis_index("dp"), ctx // NX, ctx % NX


def ctx_of(z, x):
    return {"ctx": z * NX + x}


def remote(src, dst, send, recv, device):
    return pltpu.make_async_remote_copy(
        src_ref=src, dst_ref=dst, send_sem=send, recv_sem=recv, device_id=device, device_id_type=MESH
    )


def cols(start, size):
    return pl.ds(pl.multiple_of(start, HD), size)


def rows_of(start, size):
    return pl.ds(pl.multiple_of(start, size), size)


def greet(devices):
    barrier = pltpu.get_barrier_semaphore()
    for device in devices:
        pl.semaphore_signal(barrier, inc=1, device_id=device, device_id_type=MESH)
    pl.semaphore_wait(barrier, len(devices))


def spread_kernel(
    text, dout, image, meta, q, do, kvw, images, metas,
    own_sem, x_send, x_recv, kv_send, kv_recv, up_send, up_recv, down_send, down_recv,
):
    _, z, x = place()
    up, down = (z + 1) % NZ, (z + NZ - 1) % NZ
    me = z * NX + x
    greet([ctx_of(z, (x + d) % NX) for d in (1, 2, 3)] + [ctx_of(up, x), ctx_of(down, x)])

    def pieces(head):
        return [
            (meta, metas.at[me]),
            (image.at[head], images.at[me]),
            (text.at[:, cols(NX * QC + head * HD, HD)], kvw.at[WIN - 1, rows_of(x * TOK, TOK), pl.ds(0, HD)]),
            (text.at[:, cols(NX * QC + (NX + head) * HD, HD)], kvw.at[WIN - 1, rows_of(x * TOK, TOK), pl.ds(HD, HD)]),
            (text.at[:, cols(head * QC, QC)], q.at[rows_of(x * TOK, TOK)]),
            (dout.at[:, cols(head * QC, QC)], do.at[rows_of(x * TOK, TOK)]),
        ]

    own = [pltpu.make_async_copy(src, dst, own_sem.at[k]) for k, (src, dst) in enumerate(pieces(x))]
    sent = []
    for d in (1, 2, 3):
        peer = (x + d) % NX
        sent.append([
            remote(src, dst, x_send.at[d - 1, k], x_recv.at[d - 1, k], ctx_of(z, peer))
            for k, (src, dst) in enumerate(pieces(peer))
        ])
    for k in range(6):
        own[k].start()
        for d in range(3):
            sent[d][k].start()

    def arrived(k):
        own[k].wait()
        for d in range(3):
            sent[d][k].wait_recv()

    ups, downs, kvs = [], [], []
    for k in range(4):
        block = pl.ds(((z + NZ - k) % NZ) * NX, NX)
        ups.append([
            remote(a.at[block], a.at[block], up_send.at[k, j], up_recv.at[k, j], ctx_of(up, x))
            for j, a in enumerate((metas, images))
        ])
    for k in range(3):
        block = pl.ds(((z + k) % NZ) * NX, NX)
        downs.append([
            remote(a.at[block], a.at[block], down_send.at[k, j], down_recv.at[k, j], ctx_of(down, x))
            for j, a in enumerate((metas, images))
        ])
    for k in range(5):
        part = pl.ds(0, ROW) if k < 4 else pl.ds(ROW - TOK, TOK)
        kvs.append(
            remote(kvw.at[WIN - 1 - k, part], kvw.at[WIN - 2 - k, part], kv_send.at[k], kv_recv.at[k], ctx_of(up, x))
        )

    arrived(2)
    arrived(3)

    @pl.when(z <= NZ - 2)
    def _():
        kvs[0].start()

    arrived(0)
    arrived(1)
    for j in range(2):
        ups[0][j].start()
        downs[0][j].start()
    for k in range(1, 5):

        @pl.when(z >= k)
        def _():
            kvs[k - 1].wait_recv()

        @pl.when((z >= k) & (z <= NZ - 2))
        def _():
            kvs[k].start()

        for j in range(2):
            ups[k - 1][j].wait_recv()
            if k < 4:
                ups[k][j].start()
        if k <= 3:
            for j in range(2):
                downs[k - 1][j].wait_recv()
                if k < 3:
                    downs[k][j].start()

    @pl.when(z >= 5)
    def _():
        kvs[4].wait_recv()

    arrived(4)
    arrived(5)
    for k in range(5):

        @pl.when((z >= k) & (z <= NZ - 2))
        def _():
            kvs[k].wait_send()

    for group in sent + ups + downs:
        for copy in group:
            copy.wait_send()


def attend_kernel(
    q, do, kvw, images, docs, tgt_row, tgt_col, proj,
    attn, dqm, dkv_out, scatq, sums, onehot_t, keep, rawkv,
    raw, adapted, qm, dq, ks, vs, kts, vts, s_buf, p_buf, o_acc, dkv,
):
    _, z, x = place()
    base = z * ROW
    scale = proj[pl.ds(x, 1), :]
    shift = proj[pl.ds(NX + x, 1), :]
    for pair in range(NSLOT // 16):
        first = images[2 * pair].astype(F32)
        second = images[2 * pair + 1].astype(F32)
        left = jnp.concatenate([first[:8], second[:8]], axis=0)
        right = jnp.concatenate([first[8:], second[8:]], axis=0)
        at = pl.ds(pair * 16, 16)
        raw[at, pl.ds(0, HALF)] = left.astype(BF16)
        raw[at, pl.ds(HALF, HALF)] = right.astype(BF16)
        adapted[at, pl.ds(0, HALF)] = (left * scale[:, :HALF] + shift[:, :HALF]).astype(BF16)
        adapted[at, pl.ds(HALF, HALF)] = (right * scale[:, HALF:] + shift[:, HALF:]).astype(BF16)
    rawkv[...] = raw[:, QC:]

    target = tgt_row[...]

    def chosen(begin):
        position = begin + lax.broadcasted_iota(jnp.int32, (ROW, NSLOT), 0)
        hit = jnp.where(position == target, 1.0, 0.0).astype(F32)
        return hit.astype(BF16), jnp.max(hit, axis=1, keepdims=True)

    hit, is_image = chosen(base)
    keep[...] = jnp.broadcast_to(1.0 - is_image, keep.shape)
    onehot_t[...] = jnp.where(
        tgt_col[...] == base + lax.broadcasted_iota(jnp.int32, (NSLOT, ROW), 1), 1.0, 0.0
    ).astype(BF16)
    picked = jnp.dot(hit, adapted[:, :QC], preferred_element_type=F32)
    qm[...] = jnp.where(is_image > 0.0, picked, q[...].astype(F32)).astype(BF16)

    all_docs = docs[...]
    own_docs = docs[pl.ds(z * NX, NX), :]
    own_docs = jnp.concatenate([own_docs[k : k + 1] for k in range(NX)], axis=1)
    doc_start = jnp.zeros((1, ROW), jnp.int32)
    for doc in range(1, DOCS):
        before = jnp.sum((all_docs < doc).astype(jnp.int32))
        doc_start = jnp.where(own_docs == doc, before, doc_start)
    first_key = jnp.min(doc_start)
    low = jnp.maximum((first_key - (base - (WIN - 1) * ROW)) // ROW, 0)
    low = jnp.maximum(low, WIN - 1 - z)

    dkv[...] = jnp.zeros_like(dkv)

    def place_keys(s, _):
        hit, is_image = chosen(base + (s - (WIN - 1)) * ROW)
        picked = jnp.dot(hit, adapted[:, QC:], preferred_element_type=F32)
        old = kvw[s].astype(F32)
        if True:
            live = (s > 0) | (lax.broadcasted_iota(jnp.int32, (ROW, 1), 0) >= ROW - TOK)
            old = jnp.where(live, old, 0.0)
        both = jnp.where(is_image > 0.0, picked, old)
        ks[s] = both[:, :HD].astype(BF16)
        vs[s] = both[:, HD:].astype(BF16)
        kts[s] = both[:, :HD].T.astype(BF16)
        vts[s] = both[:, HD:].T.astype(BF16)
        return 0

    lax.fori_loop(low, WIN, place_keys, 0)

    query_pos = base + lax.broadcasted_iota(jnp.int32, (1, ROW), 1)

    def head(r, _):
        at = cols(r * HD, HD)
        q_t = qm[:, at].astype(F32).T
        do_t = do[:, at].astype(F32).T
        q_tb = q_t.astype(BF16)
        do_tb = do_t.astype(BF16)

        def scores(s, top):
            key_pos = base + (s - (WIN - 1)) * ROW + lax.broadcasted_iota(jnp.int32, (ROW, 1), 0)
            value = jnp.dot(ks[s], q_tb, preferred_element_type=F32) * (SCALE * LOG2E)
            value = jnp.where((key_pos >= doc_start) & (key_pos <= query_pos), value, -1e30)
            s_buf[s] = value
            return jnp.maximum(top, jnp.max(value.reshape(ROW // 8, 8, ROW), axis=0))

        top = lax.fori_loop(low, WIN, scores, jnp.full((8, ROW), -1e30, F32))
        top = jnp.max(top, axis=0, keepdims=True)
        o_acc[...] = jnp.zeros_like(o_acc)

        def weigh(s, total):
            value = jnp.exp2(s_buf[s] - top)
            value_b = value.astype(BF16)
            p_buf[s] = value_b
            o_acc[...] += jnp.dot(vts[s], value_b, preferred_element_type=F32)
            return total + jnp.sum(value.reshape(ROW // 8, 8, ROW), axis=0)

        total = lax.fori_loop(low, WIN, weigh, jnp.zeros((8, ROW), F32))
        inverse = 1.0 / jnp.sum(total, axis=0, keepdims=True)
        out_t = (o_acc[...] * inverse).astype(BF16).astype(F32)
        attn[:, at] = out_t.T.astype(BF16)
        corr = jnp.sum(do_t * out_t, axis=0, keepdims=True)
        q_n = (q_t * (inverse * SCALE)).T.astype(BF16)
        do_n = (do_t * inverse).T.astype(BF16)
        o_acc[...] = jnp.zeros_like(o_acc)

        def back(s, _):
            prob = p_buf[s]
            dprob = jnp.dot(vs[s], do_tb, preferred_element_type=F32)
            dscore = (prob.astype(F32) * (dprob - corr)).astype(BF16)
            o_acc[...] += jnp.dot(kts[s], dscore, preferred_element_type=F32)
            dkv[s, :, :HD] += jnp.dot(dscore, q_n, preferred_element_type=F32)
            dkv[s, :, HD:] += jnp.dot(prob, do_n, preferred_element_type=F32)
            return 0

        lax.fori_loop(low, WIN, back, 0)
        dq[:, at] = (o_acc[...] * (inverse * SCALE)).T.astype(BF16)
        return 0

    lax.fori_loop(0, REP, head, 0)

    dkv_out[...] = dkv[...].astype(BF16)
    dqm[...] = jnp.where(is_image > 0.0, 0.0, dq[...].astype(F32)).astype(BF16)
    scattered = jnp.dot(onehot_t[...], dq[...], preferred_element_type=F32)
    scatq[...] = scattered.astype(BF16)
    scale_part = jnp.sum(scattered * raw[:, :QC].astype(F32), axis=0, keepdims=True)
    shift_part = jnp.sum(scattered, axis=0, keepdims=True)
    sums[...] = jnp.zeros_like(sums)
    for k in range(REP):
        sums[pl.ds(k, 1), :] = scale_part[:, k * HD : (k + 1) * HD]
        sums[pl.ds(10 + k, 1), :] = shift_part[:, k * HD : (k + 1) * HD]


def return_kernel(
    attn, dqm, part, scatq, sums_in, onehot_t, keep, rawkv, proj,
    attn_out, text_grad, image_out, sums_out,
    first_in, ring_in, ring_out, dkv, mkv, scatkv, rxq, rxkv, igs, vec, vec_z, vec_x, r_dp, r_z, r_x,
    own_sem, x_send, x_recv, ring_send, ring_recv, z_send, z_recv, dp_send, dp_recv,
):
    dp, z, x = place()
    up, down = (z + 1) % NZ, (z + NZ - 1) % NZ
    greet(
        [ctx_of(z, (x + d) % NX) for d in (1, 2, 3)]
        + [ctx_of((z + d) % NZ, x) for d in range(1, NZ)]
        + [{"dp": (dp + d) % NDP} for d in range(1, NDP)]
    )

    head = remote(
        part.at[0, pl.ds(ROW - TOK, TOK)], first_in, ring_send.at[0], ring_recv.at[0], ctx_of(down, x)
    )

    @pl.when(z >= WIN - 1)
    def _():
        head.start()

    def row_pieces(peer):
        return [
            (attn.at[rows_of(peer * TOK, TOK)], attn_out.at[:, cols(x * QC, QC)]),
            (dqm.at[rows_of(peer * TOK, TOK)], text_grad.at[:, cols(x * QC, QC)]),
            (mkv.at[rows_of(peer * TOK, TOK), pl.ds(0, HD)], text_grad.at[:, cols(NX * QC + x * HD, HD)]),
            (mkv.at[rows_of(peer * TOK, TOK), pl.ds(HD, HD)], text_grad.at[:, cols(NX * QC + (NX + x) * HD, HD)]),
            (igs.at[peer], image_out.at[x]),
            (vec_x, r_x.at[x]),
        ]

    own = [pltpu.make_async_copy(src, dst, own_sem.at[k]) for k, (src, dst) in enumerate(row_pieces(x))]
    sent = []
    for d in (1, 2, 3):
        peer = (x + d) % NX
        sent.append([
            remote(src, dst, x_send.at[d - 1, k], x_recv.at[d - 1, k], ctx_of(z, peer))
            for k, (src, dst) in enumerate(row_pieces(peer))
        ])

    def send_x(k):
        for d in range(3):
            sent[d][k].start()
        own[k].start()

    def arrived_x(k):
        own[k].wait()
        for d in range(3):
            sent[d][k].wait_recv()

    def z_pieces(peer):
        return [
            (scatq.at[rows_of(peer * 32, 32)], rxq.at[z]),
            (scatkv.at[rows_of(peer * 32, 32)], rxkv.at[z]),
            (vec_z, r_z.at[z]),
        ]

    own_z = [pltpu.make_async_copy(src, dst, own_sem.at[6 + k]) for k, (src, dst) in enumerate(z_pieces(z))]
    sent_z = []
    for d in range(1, NZ):
        peer = (z + d) % NZ
        sent_z.append([
            remote(src, dst, z_send.at[d - 1, k], z_recv.at[d - 1, k], ctx_of(peer, x))
            for k, (src, dst) in enumerate(z_pieces(peer))
        ])

    def send_z(k):
        for d in range(NZ - 1):
            sent_z[d][k].start()
        own_z[k].start()

    def arrived_z(k):
        own_z[k].wait()
        for d in range(NZ - 1):
            sent_z[d][k].wait_recv()

    send_x(0)
    send_x(1)
    send_z(0)

    ring = [
        remote(ring_out.at[k], ring_in.at[k], ring_send.at[1 + k], ring_recv.at[1 + k], ctx_of(down, x))
        for k in range(4)
    ]
    for s in range(1, WIN - 1):

        @pl.when(z >= WIN - 1 - s)
        def _():
            @pl.when(z == NZ - 1)
            def _():
                ring_out[s - 1] = part[s]

            @pl.when(z <= NZ - 2)
            def _():
                if s == 1:
                    head.wait_recv()
                    ring_out[0, : ROW - TOK] = part[s, : ROW - TOK]
                    ring_out[0, ROW - TOK :] = (
                        part[s, ROW - TOK :].astype(F32) + first_in[...].astype(F32)
                    ).astype(BF16)
                else:
                    ring[s - 2].wait_recv()
                    ring_out[s - 1] = (part[s].astype(F32) + ring_in[s - 2].astype(F32)).astype(BF16)

            ring[s - 1].start()

    @pl.when(z == NZ - 1)
    def _():
        dkv[...] = part[WIN - 1]

    @pl.when(z <= NZ - 2)
    def _():
        ring[3].wait_recv()
        dkv[...] = (part[WIN - 1].astype(F32) + ring_in[3].astype(F32)).astype(BF16)

    whole = dkv[...]
    kept = keep[...]
    mkv[...] = (whole.astype(F32) * jnp.concatenate([kept, kept], axis=1)).astype(BF16)
    send_x(2)
    send_x(3)
    scattered = jnp.dot(onehot_t[...], whole, preferred_element_type=F32)
    scatkv[...] = scattered.astype(BF16)
    send_z(1)
    scale_part = jnp.sum(scattered * rawkv[...].astype(F32), axis=0, keepdims=True)
    shift_part = jnp.sum(scattered, axis=0, keepdims=True)
    vec[...] = sums_in[...]
    for k in range(2):
        vec[pl.ds(REP + k, 1), :] = scale_part[:, k * HD : (k + 1) * HD]
        vec[pl.ds(10 + REP + k, 1), :] = shift_part[:, k * HD : (k + 1) * HD]
    own_dp = pltpu.make_async_copy(vec, r_dp.at[dp], own_sem.at[9])
    sent_dp = [
        remote(vec, r_dp.at[dp], dp_send.at[d - 1], dp_recv.at[d - 1], {"dp": (dp + d) % NDP}) for d in range(1, NDP)
    ]
    for copy in sent_dp:
        copy.start()
    own_dp.start()

    arrived_z(0)
    arrived_z(1)
    scale = proj[pl.ds(x, 1), :]
    slots_q = rxq[0].astype(F32)
    slots_kv = rxkv[0].astype(F32)
    for k in range(1, NZ):
        slots_q = slots_q + rxq[k].astype(F32)
        slots_kv = slots_kv + rxkv[k].astype(F32)
    grad = jnp.concatenate([slots_q, slots_kv], axis=1) * scale
    for k in range(NX):
        piece = grad[k * SLOTS : (k + 1) * SLOTS]
        igs[k] = jnp.concatenate([piece[:, :HALF], piece[:, HALF:]], axis=0).astype(BF16)
    send_x(4)

    own_dp.wait()
    for copy in sent_dp:
        copy.wait_recv()
    value = r_dp[0]
    for k in range(1, NDP):
        value = value + r_dp[k]
    vec_z[...] = value
    send_z(2)
    arrived_z(2)
    value = r_z[0]
    for k in range(1, NZ):
        value = value + r_z[k]
    vec_x[...] = value
    send_x(5)
    arrived_x(5)
    sums_out[...] = r_x[...]
    for k in range(5):
        arrived_x(k)

    @pl.when(z >= WIN - 1)
    def _():
        head.wait_send()

    for s in range(1, WIN - 1):

        @pl.when(z >= WIN - 1 - s)
        def _():
            ring[s - 1].wait_send()

    for group in sent + sent_z:
        for copy in group:
            copy.wait_send()
    for copy in sent_dp:
        copy.wait_send()


def by_head(a):
    lead = a.shape[:-1]
    parts = [
        a[..., : NX * QC].reshape(*lead, NX, QC),
        a[..., NX * QC : NX * (QC + HD)].reshape(*lead, NX, HD),
        a[..., NX * (QC + HD) :].reshape(*lead, NX, HD),
    ]
    return jnp.concatenate(parts, axis=-1)


def from_heads(a):
    lead = a.shape[:-2]
    parts = [a[..., :QC], a[..., QC : QC + HD], a[..., QC + HD :]]
    return jnp.concatenate([part.reshape(*lead, -1) for part in parts], axis=-1)


def shape(dims, kind):
    return jax.ShapeDtypeStruct(dims, kind)


ANY = pl.BlockSpec(memory_space=pl.ANY)
VMEM = pl.BlockSpec(memory_space=pltpu.VMEM)
DMA = pltpu.SemaphoreType.DMA
LIMIT = 56 * 1024 * 1024


def per_device(
    text_rows, image_rows, tile_counts, tile_offsets, doc_ids, out_grad, proj_scale, proj_shift
):
    image = by_head(image_rows[0]).reshape(SLOTS, NX, 2, HALF)
    image = image.transpose(1, 2, 0, 3).reshape(NX, 16, HALF)
    slot = jnp.arange(TOK, dtype=jnp.int32)
    target = jnp.where(slot < tile_counts[0, 0], tile_offsets[0, 0] + slot, -(1 << 20))
    meta = jnp.concatenate([doc_ids, target[None], jnp.zeros((6, TOK), jnp.int32)], axis=0)
    proj = jnp.concatenate([by_head(proj_scale), by_head(proj_shift)], axis=0)

    q, do, kvw, images, metas = pl.pallas_call(
        spread_kernel,
        out_shape=(
            shape((ROW, QC), BF16),
            shape((ROW, QC), BF16),
            shape((WIN, ROW, 2 * HD), BF16),
            shape((NZ * NX, 16, HALF), BF16),
            shape((NZ * NX, 8, TOK), jnp.int32),
        ),
        in_specs=[ANY] * 4,
        out_specs=(ANY,) * 5,
        scratch_shapes=[
            DMA((6,)), DMA((3, 6)), DMA((3, 6)), DMA((5,)), DMA((5,)),
            DMA((4, 2)), DMA((4, 2)), DMA((3, 2)), DMA((3, 2)),
        ],
        compiler_params=pltpu.CompilerParams(collective_id=0, has_side_effects=True),
        name="spread",
    )(text_rows[0], out_grad[0], image, meta)

    docs = metas[:, 0, :]
    targets = metas[:, 1, :SLOTS].reshape(NSLOT)

    attn, dqm, part, scatq, sums, onehot_t, keep, rawkv = pl.pallas_call(
        attend_kernel,
        out_shape=(
            shape((ROW, QC), BF16),
            shape((ROW, QC), BF16),
            shape((WIN, ROW, 2 * HD), BF16),
            shape((NSLOT, QC), BF16),
            shape((24, HD), F32),
            shape((NSLOT, ROW), BF16),
            shape((ROW, HD), F32),
            shape((NSLOT, 2 * HD), BF16),
        ),
        in_specs=[VMEM] * 8,
        out_specs=(VMEM,) * 8,
        scratch_shapes=[
            pltpu.VMEM((NSLOT, HC), BF16),
            pltpu.VMEM((NSLOT, HC), BF16),
            pltpu.VMEM((ROW, QC), BF16),
            pltpu.VMEM((ROW, QC), BF16),
            pltpu.VMEM((WIN, ROW, HD), BF16),
            pltpu.VMEM((WIN, ROW, HD), BF16),
            pltpu.VMEM((WIN, HD, ROW), BF16),
            pltpu.VMEM((WIN, HD, ROW), BF16),
            pltpu.VMEM((WIN, ROW, ROW), F32),
            pltpu.VMEM((WIN, ROW, ROW), BF16),
            pltpu.VMEM((HD, ROW), F32),
            pltpu.VMEM((WIN, ROW, 2 * HD), F32),
        ],
        compiler_params=pltpu.CompilerParams(vmem_limit_bytes=LIMIT),
        name="attend",
    )(q, do, kvw, images, docs, targets[None, :], targets[:, None], proj)

    attn_out, text_grad, image_out, sums = pl.pallas_call(
        return_kernel,
        out_shape=(
            shape((TOK, NX * QC), BF16),
            shape((TOK, NX * HC), BF16),
            shape((NX, 16, HALF), BF16),
            shape((NX, 24, HD), F32),
        ),
        in_specs=[ANY, ANY, VMEM, VMEM, VMEM, VMEM, VMEM, VMEM, VMEM],
        out_specs=(ANY, ANY, ANY, VMEM),
        scratch_shapes=[
            pltpu.VMEM((TOK, 2 * HD), BF16),
            pltpu.VMEM((4, ROW, 2 * HD), BF16),
            pltpu.VMEM((4, ROW, 2 * HD), BF16),
            pltpu.VMEM((ROW, 2 * HD), BF16),
            pltpu.VMEM((ROW, 2 * HD), BF16),
            pltpu.VMEM((NSLOT, 2 * HD), BF16),
            pltpu.VMEM((NZ, 32, QC), BF16),
            pltpu.VMEM((NZ, 32, 2 * HD), BF16),
            pltpu.VMEM((NX, 16, HALF), BF16),
            pltpu.VMEM((24, HD), F32),
            pltpu.VMEM((24, HD), F32),
            pltpu.VMEM((24, HD), F32),
            pltpu.VMEM((NDP, 24, HD), F32),
            pltpu.VMEM((NZ, 24, HD), F32),
            pltpu.VMEM((NX, 24, HD), F32),
            DMA((10,)), DMA((3, 6)), DMA((3, 6)), DMA((5,)), DMA((5,)),
            DMA((7, 3)), DMA((7, 3)), DMA((7,)), DMA((7,)),
        ],
        compiler_params=pltpu.CompilerParams(
            collective_id=1, has_side_effects=True, vmem_limit_bytes=LIMIT
        ),
        name="give_back",
    )(attn, dqm, part, scatq, sums, onehot_t, keep, rawkv, proj)

    image_grad = image_out.reshape(NX, 2, SLOTS, HALF).transpose(2, 0, 1, 3).reshape(SLOTS, NX, HC)
    image_grad = from_heads(image_grad)[None]
    scale_grad = from_heads(sums[:, :10].reshape(NX, HC))
    shift_grad = from_heads(sums[:, 10:20].reshape(NX, HC))
    return (attn_out[None], text_grad[None], image_grad, scale_grad, shift_grad)


def solution(mesh):
    return jax.shard_map(
        per_device,
        mesh=mesh,
        in_specs=(
            P("dp", "ctx", None),
            P("dp", "ctx", None),
            P("dp", "ctx"),
            P("dp", "ctx"),
            P("dp", "ctx"),
            P("dp", "ctx", None),
            P(),
            P(),
        ),
        out_specs=(P("dp", "ctx", None), P("dp", "ctx", None), P("dp", "ctx", None), P(), P()),
        check_vma=False,
    )
```

time: 893 us -> 213 us (0.24)
  waiting for transfers between devices: 692 us -> 0 us
  Pallas kernels: 0 us -> 192 us
  blocking collectives: 97.4 us -> 0 us
  local copies, waits for them, and re-layouts: 50.5 us -> 13.6 us
  matrix products: 17 us -> 0 us
  between operations: 15.3 us -> 2.02 us
  other arithmetic: 16.3 us -> 4.45 us
    unnamed x5 -> x0, waiting for transfers between devices: 332 us -> none
    reduce_scatter x1 -> x0, waiting for transfers between devices: 212 us -> none  [per_device(): lax.psum_scatter(scattered.astype(jnp.bfloat16), 'ctx', scatter_dimension...]
    pallas_call x0 -> x3, Pallas kernels: none -> 192 us  [the longest x1 126 us: per_device(): pl.pallas_call(return_kernel, out_shape=(shape((TOK, NX * QC), BF16), sha...]
    all_gather x2 -> x0, waiting for transfers between devices: 148 us -> none  [the longest x1 90.6 us: per_device(): lax.all_gather(keyval, 'ctx', axis=0, tiled=True)]
    psum x2 -> x0, blocking collectives: 97.4 us -> none  [the longest x1 74 us: per_device(): scale_grad, shift_grad = lax.psum((scale_part, shift_part), ('dp', 'ctx'))]
    unnamed x27 -> x11, local copies, waits for them, and re-layouts: 31.6 us -> 4.26 us
    dot_general x8 -> x0, matrix products: 17 us -> none  [the longest x1 3.09 us: backward_step(): jnp.einsum('pgrd,tgd->grpt', dout, vals, preferred_element_type=jnp.float32)]
  transfers between devices with their start and end apart: 4 -> 0, of which waited for: 4 -> 0; matrix products, arithmetic and copies ran while one was open for 1% -> 0% of each run, Pallas kernels for 0% -> 0%
where the time goes in v1:
time: 213 us; the launch traced here: 212 us
  Pallas kernels  192 us (90%)
  local copies, waits for them, and re-layouts  13.6 us (6%)
  other arithmetic  4.45 us (2%)
    pallas_call x1, Pallas kernels, per_device(): pl.pallas_call(return_kernel, out_shape=(shape((TOK, NX * QC), BF16), sha...  126 us
    pallas_call x1, Pallas kernels, per_device(): pl.pallas_call(spread_kernel, out_shape=(shape((ROW, QC), BF16), shape((R...  44.8 us
    pallas_call x1, Pallas kernels, per_device(): pl.pallas_call(attend_kernel, out_shape=(shape((ROW, QC), BF16), shape((R...  21.5 us
    unnamed x11, local copies, waits for them, and re-layouts  4.26 us

profile of v1, /device:TPU:8, one launch (start us, length us, event | category | flops | bytes accessed | tf_op | source)
XLA Modules:
  0.0 212.1 jit_solution(7728921953903167644)
XLA Ops:
  2.0 1.3 add_add_fusion.meta
  3.3 0.8 slice_bitcast_fusion.14
  4.1 0.7 slice.131
  4.8 0.7 slice.137
  5.6 0.6 maximum_maximum_fusion.proj
  6.2 0.7 slice_bitcast_fusion.8
  6.9 0.8 slice.154
  7.8 0.6 pad_maximum_fusion
  8.4 44.8 %spread.1 = (bf16[512,1024]{1,0:T(8,128)(2,1)}, bf16[512,1024]{1,0:T(8,128)(2,1)}, bf16[6,512,256]{2,1,0:T(8,128)(2,1)}, bf16[32,16,640]{2,1,0:T(8,128)(2,1)}, s32[32,8,128]{2,1,0:T(8,128)}) custom-call(bf16[128,5120]{1,0:T(8,128)(2,1)} %bitcast.70, bf16[128,4096]{1,0:T(8,128)(2,1)} %bitcast.72, bf16[4,16,640]{2,1,0:T(8,128)(2,1)} %bitcast.74, ...), custom_call_target="tpu_custom_call" | custom-call | tf_op jit(solution)/shard_map/spread/pallas_call | solution.py:519
  53.2 1.0 fusion
  54.1 0.9 copy.14
  55.1 0.6 slice_bitcast_fusion.4.docs
  55.7 0.7 broadcast_in_dim_reshape_squeeze.6.tgt_row
  56.3 0.8 broadcast_in_dim_reshape_squeeze.8.tgt_col
  57.1 21.5 %attend.1 = (bf16[512,1024]{1,0:T(8,128)(2,1)}, bf16[512,1024]{1,0:T(8,128)(2,1)}, bf16[6,512,256]{2,1,0:T(8,128)(2,1)}, bf16[256,1024]{1,0:T(8,128)(2,1)}, f32[...) custom-call(bf16[512,1024]{1,0:T(8,128)(2,1)} %get-tuple-element.22.q, ...), custom_call_target="tpu_custom_call" | custom-call | tf_op jit(solution)/shard_map/attend/pallas_call | solution.py:541
  78.6 125.7 %give_back.1 = (bf16[128,4096]{1,0:T(8,128)(2,1)}, bf16[128,5120]{1,0:T(8,128)(2,1)}, bf16[4,16,640]{2,1,0:T(8,128)(2,1)}, f32[4,24,128]{2,1,0:T(8,128)}) custom-call(bf16[512,1024]{1,0:T(8,128)(2,1)} %get-tuple-element.27.attn, bf16[512,1024]{1,0:T(8,128)(2,1)} %get-tuple-element.28.dqm, bf16[6,512,256]{2,1,0:T(8,128)(2,1)} %get-tuple-element.29.part, ...), custom_call_target="tpu_custom_call" | custom-call | tf_op jit(solution)/shard_map/give_back/pallas_call | solution.py:573
  204.3 0.7 slice_bitcast_fusion.6
  205.0 0.8 slice.158
  205.9 0.6 maximum_bitcast_fusion
  206.5 0.9 slice_bitcast_fusion
  207.5 0.6 pad_maximum_fusion.2
  208.1 0.6 pad_maximum_fusion.1
  208.7 2.3 %copy.32 = bf16[1,128,4096]{2,1,0:T(8,128)(2,1)} copy(bf16[1,128,4096]{2,1,0:T(8,128)(2,1)} %bitcast.73) | data formatting | bytes 2097152
  211.0 1.1 copy.33
  (15 shorter events, 0.2 us)
Async XLA Ops:
  206.5 4.5 %copy-start = (bf16[128,5120]{1,0:T(8,128)(2,1)S(1)}, bf16[128,5120]{1,0:T(8,128)(2,1)}, u32[]{:S(2)}) copy-start(bf16[128,5120]{1,0:T(8,128)(2,1)} %get-tuple-element.36) | copy-start | bytes 3932164

commit v2 on v0

v2 whole, which is shorter than its diff:
```python
import math

import jax
import jax.numpy as jnp
from jax import lax
from jax.experimental import pallas as pl
from jax.experimental.pallas import tpu as pltpu
from jax.sharding import PartitionSpec as P

MESH = pl.DeviceIdType.MESH
HD = 128
REP = 8
DOCS = 8
NZ = 8
NX = 4
NDP = 8
TOK = 128
ROW = NX * TOK
SLOTS = 8
NSLOT = NZ * NX * SLOTS
QC = REP * HD
HC = QC + 2 * HD
WIN = 6
HALF = HC // 2
LANES = REP * TOK
SCALE = HD ** -0.5
LOG2E = math.log2(math.e)
F32 = jnp.float32
BF16 = jnp.bfloat16


def place():
    ctx = lax.axis_index("ctx")
    return lax.axis_index("dp"), ctx // NX, ctx % NX


def ctx_of(z, x):
    return {"ctx": z * NX + x}


def remote(src, dst, send, recv, device):
    return pltpu.make_async_remote_copy(
        src_ref=src, dst_ref=dst, send_sem=send, recv_sem=recv, device_id=device, device_id_type=MESH
    )


def cols(start, size):
    return pl.ds(pl.multiple_of(start, HD), size)


def rows_of(start, size):
    return pl.ds(pl.multiple_of(start, size), size)


def greet(devices):
    barrier = pltpu.get_barrier_semaphore()
    for device in devices:
        pl.semaphore_signal(barrier, inc=1, device_id=device, device_id_type=MESH)
    pl.semaphore_wait(barrier, len(devices))


def layer_kernel(
    text, dout, image, meta, proj,
    attn_out, text_grad, image_out, sums_out,
    q_in, do_in, kvw, images, metas, raw, adapted, onehot_t, keep, starts,
    q_t, do_t, q_s, do_s, ks, vs, kts, vts, p_buf, p_first, acc_t, top, total, tops, corr, dkv,
    attn, dq, first_in, first_out, ring_in, ring_out, whole, mkv, scatq, scatkv, rxq, rxkv, igs,
    vec, vec_z, vec_x, r_dp, r_z, r_x,
    own_sem, x_send, x_recv, kv_send, kv_recv, up_send, up_recv, down_send, down_recv,
    ring_send, ring_recv, z_send, z_recv, dp_send, dp_recv,
):
    dp, z, x = place()
    up, down = (z + 1) % NZ, (z + NZ - 1) % NZ
    me = z * NX + x
    base = z * ROW
    greet(
        [ctx_of(z, (x + d) % NX) for d in range(1, NX)]
        + [ctx_of((z + d) % NZ, x) for d in range(1, NZ)]
        + [{"dp": (dp + d) % NDP} for d in range(1, NDP)]
    )

    def pieces(peer):
        own_rows = rows_of(x * TOK, TOK)
        return [
            (meta, metas.at[me]),
            (image.at[peer], images.at[me]),
            (text.at[:, cols(NX * QC + peer * HD, HD)], kvw.at[WIN - 1, own_rows, pl.ds(0, HD)]),
            (text.at[:, cols(NX * QC + (NX + peer) * HD, HD)], kvw.at[WIN - 1, own_rows, pl.ds(HD, HD)]),
            (text.at[:, cols(peer * QC, QC)], q_in.at[x]),
            (dout.at[:, cols(peer * QC, QC)], do_in.at[x]),
            (attn.at[peer], attn_out.at[:, cols(x * QC, QC)]),
            (dq.at[peer], text_grad.at[:, cols(x * QC, QC)]),
            (mkv.at[rows_of(peer * TOK, TOK), pl.ds(0, HD)], text_grad.at[:, cols(NX * QC + x * HD, HD)]),
            (mkv.at[rows_of(peer * TOK, TOK), pl.ds(HD, HD)], text_grad.at[:, cols(NX * QC + (NX + x) * HD, HD)]),
            (igs.at[peer], image_out.at[x]),
            (vec_x, r_x.at[x]),
        ]

    own_x = [pltpu.make_async_copy(src, dst, own_sem.at[k]) for k, (src, dst) in enumerate(pieces(x))]
    sent_x = []
    for d in range(1, NX):
        peer = (x + d) % NX
        sent_x.append([
            remote(src, dst, x_send.at[d - 1, k], x_recv.at[d - 1, k], ctx_of(z, peer))
            for k, (src, dst) in enumerate(pieces(peer))
        ])

    def send_x(k):
        for d in range(NX - 1):
            sent_x[d][k].start()
        own_x[k].start()

    def arrived_x(k):
        own_x[k].wait()
        for d in range(NX - 1):
            sent_x[d][k].wait_recv()

    for k in range(6):
        send_x(k)

    ups, downs = [], []
    for k in range(3):
        block = pl.ds(((z + NZ - k) % NZ) * NX, NX)
        ups.append([
            remote(a.at[block], a.at[block], up_send.at[k, j], up_recv.at[k, j], ctx_of(up, x))
            for j, a in enumerate((metas, images))
        ])
    for k in range(4):
        block = pl.ds(((z + k) % NZ) * NX, NX)
        downs.append([
            remote(a.at[block], a.at[block], down_send.at[k, j], down_recv.at[k, j], ctx_of(down, x))
            for j, a in enumerate((metas, images))
        ])

    def passed(k):
        return remote(
            kvw.at[WIN - 1 - k], kvw.at[WIN - 2 - k], kv_send.at[k], kv_recv.at[k], ctx_of(up, x)
        )

    tail = pl.ds(ROW - TOK, TOK)
    last = remote(kvw.at[1, tail], kvw.at[0, tail], kv_send.at[4], kv_recv.at[4], ctx_of(up, x))

    arrived_x(0)
    arrived_x(1)
    for j in range(2):
        ups[0][j].start()
        downs[0][j].start()
    arrived_x(2)
    arrived_x(3)

    @pl.when(z <= NZ - 2)
    def _():
        passed(0).start()

    for k in range(1, 5):
        for j in range(2):
            if k <= 3:
                ups[k - 1][j].wait_recv()
            if k < 3:
                ups[k][j].start()
            downs[k - 1][j].wait_recv()
            if k < 4:
                downs[k][j].start()

    scale = proj[pl.ds(x, 1), :]
    shift = proj[pl.ds(NX + x, 1), :]

    def adapt(pair, _):
        first = images[2 * pair].astype(F32)
        second = images[2 * pair + 1].astype(F32)
        left = jnp.concatenate([first[:8], second[:8]], axis=0)
        right = jnp.concatenate([first[8:], second[8:]], axis=0)
        at = rows_of(pair * 16, 16)
        raw[at, pl.ds(0, HALF)] = left.astype(BF16)
        raw[at, pl.ds(HALF, HALF)] = right.astype(BF16)
        adapted[at, pl.ds(0, HALF)] = (left * scale[:, :HALF] + shift[:, :HALF]).astype(BF16)
        adapted[at, pl.ds(HALF, HALF)] = (right * scale[:, HALF:] + shift[:, HALF:]).astype(BF16)
        return 0

    lax.fori_loop(0, NSLOT // 16, adapt, 0)
    all_metas = jnp.sum(metas[:, 1:3, :], axis=0)
    target = jnp.concatenate([all_metas[0:1], all_metas[1:2]], axis=1) - 1
    all_docs = metas[:, 0, :]
    before = [
        jnp.sum(jnp.where(all_docs < doc, 1, 0).astype(F32), axis=(0, 1), keepdims=True).astype(jnp.int32)
        for doc in range(1, DOCS)
    ]

    def chosen(begin, size):
        position = begin + lax.broadcasted_iota(jnp.int32, (size, NSLOT), 0)
        hit = jnp.where(position == target, 1.0, 0.0).astype(F32)
        return hit, jnp.max(hit, axis=1, keepdims=True)

    arrived_x(4)

    def place_queries(a, _):
        hit, is_image = chosen(base + a * TOK, TOK)
        onehot_t[:, cols(a * TOK, TOK)] = hit.T.astype(BF16)
        keep[rows_of(a * TOK, TOK), :] = jnp.broadcast_to(1.0 - is_image, (TOK, HD))
        picked = jnp.dot(hit.astype(BF16), adapted[:, :QC], preferred_element_type=F32)
        value = jnp.where(is_image > 0.0, picked, q_in[a].astype(F32))
        for r in range(REP):
            piece = value[:, r * HD : (r + 1) * HD]
            q_s[a, r * HD : (r + 1) * HD, :] = piece.astype(BF16)
            q_t[a, :, r * HD : (r + 1) * HD] = piece.T.astype(BF16)
        docs = metas[z * NX + a, 0:1, :]
        start = jnp.zeros((1, TOK), jnp.int32)
        for doc in range(1, DOCS):
            start = jnp.where(docs == doc, before[doc - 1], start)
        starts[a] = jnp.concatenate([start] * REP, axis=1)
        top[a] = jnp.full((1, LANES), -1e30, F32)
        total[a] = jnp.zeros((1, LANES), F32)
        acc_t[a] = jnp.zeros((HD, LANES), F32)
        return 0

    lax.fori_loop(0, NX, place_queries, 0)

    def place_keys(s, at, size):
        hit, is_image = chosen(base + (s - (WIN - 1)) * ROW + at, size)
        picked = jnp.dot(hit.astype(BF16), adapted[:, QC:], preferred_element_type=F32)
        both = jnp.where(is_image > 0.0, picked, kvw[s, at : at + size].astype(F32))
        ks[s, at : at + size, :] = both[:, :HD].astype(BF16)
        vs[s, at : at + size, :] = both[:, HD:].astype(BF16)
        kts[s, :, at : at + size] = both[:, :HD].T.astype(BF16)
        vts[s, :, at : at + size] = both[:, HD:].T.astype(BF16)

    within = lax.broadcasted_iota(jnp.int32, (1, TOK), 1)
    within = jnp.concatenate([within] * REP, axis=1)

    def forward(s, a, at, size, keep_prob):
        key_pos = base + (s - (WIN - 1)) * ROW + at + lax.broadcasted_iota(jnp.int32, (size, 1), 0)
        value = jnp.dot(ks[s, at : at + size, :], q_t[a], preferred_element_type=F32) * (SCALE * LOG2E)
        value = jnp.where((key_pos >= starts[a]) & (key_pos <= base + a * TOK + within), value, -1e30)
        old = top[a]
        new = jnp.maximum(old, jnp.max(value, axis=0, keepdims=True))
        top[a] = new
        tops[s, a] = new
        factor = jnp.exp2(old - new)
        prob = jnp.exp2(value - new)
        total[a] = total[a] * factor + jnp.sum(prob, axis=0, keepdims=True)
        prob_b = prob.astype(BF16)
        keep_prob(prob_b)
        acc_t[a] = acc_t[a] * factor + jnp.dot(vts[s, :, at : at + size], prob_b, preferred_element_type=F32)

    def forward_row(k, _):
        s = WIN - 1 - k

        @pl.when(k >= 1)
        def _():
            passed(k - 1).wait_recv()

        @pl.when((k >= 1) & (k <= 3) & (z <= NZ - 2))
        def _():
            passed(k).start()

        @pl.when((k == 4) & (z <= NZ - 2))
        def _():
            last.start()

        place_keys(s, 0, ROW)

        def one(a, _):
            def keep_prob(prob):
                p_buf[s - 1, a] = prob

            forward(s, a, 0, ROW, keep_prob)
            return 0

        lax.fori_loop(0, NX, one, 0)
        return 0

    lax.fori_loop(0, jnp.minimum(z + 1, 5), forward_row, 0)

    @pl.when(z >= WIN - 1)
    def _():
        last.wait_recv()
        place_keys(0, ROW - TOK, TOK)

        def keep_prob(prob):
            p_first[...] = prob

        forward(0, 0, ROW - TOK, TOK, keep_prob)

    arrived_x(5)

    def finish(a, _):
        for r in range(REP):
            piece = do_in[a, :, r * HD : (r + 1) * HD]
            do_s[a, r * HD : (r + 1) * HD, :] = piece
            do_t[a, :, r * HD : (r + 1) * HD] = piece.astype(F32).T.astype(BF16)
        inverse = 1.0 / total[a]
        total[a] = inverse
        out_t = (acc_t[a] * inverse).astype(BF16).astype(F32)
        corr[a] = jnp.sum(do_t[a].astype(F32) * out_t, axis=0, keepdims=True)
        for r in range(REP):
            attn[a, :, r * HD : (r + 1) * HD] = out_t[:, r * HD : (r + 1) * HD].T.astype(BF16)
        acc_t[a] = jnp.zeros((HD, LANES), F32)
        return 0

    lax.fori_loop(0, NX, finish, 0)
    send_x(6)

    def backward(s, a, at, size, prob_b):
        part = jnp.exp2(tops[s, a] - top[a]) * total[a]
        prob = prob_b.astype(F32) * part
        dprob = jnp.dot(vs[s, at : at + size, :], do_t[a], preferred_element_type=F32)
        dscore = (prob * (dprob - corr[a])).astype(BF16)
        acc_t[a] += jnp.dot(kts[s, :, at : at + size], dscore, preferred_element_type=F32)
        dk = jnp.dot(dscore, q_s[a], preferred_element_type=F32)
        dv = jnp.dot(prob.astype(BF16), do_s[a], preferred_element_type=F32)
        return dk, dv

    first = remote(first_out, first_in, ring_send.at[0], ring_recv.at[0], ctx_of(down, x))
    ring = [
        remote(ring_out.at[k], ring_in.at[k], ring_send.at[1 + k], ring_recv.at[1 + k], ctx_of(down, x))
        for k in range(4)
    ]

    @pl.when(z >= WIN - 1)
    def _():
        dk, dv = backward(0, 0, ROW - TOK, TOK, p_first[...])
        first_out[:, :HD] = (dk * SCALE).astype(BF16)
        first_out[:, HD:] = dv.astype(BF16)
        first.start()

    def backward_row(s):
        def one(a, _):
            dk, dv = backward(s, a, 0, ROW, p_buf[s - 1, a])

            @pl.when(a == 0)
            def _():
                dkv[:, :HD] = dk
                dkv[:, HD:] = dv

            @pl.when(a > 0)
            def _():
                dkv[:, :HD] += dk
                dkv[:, HD:] += dv

            return 0

        lax.fori_loop(0, NX, one, 0)
        dkv[:, :HD] = dkv[:, :HD] * SCALE

    def add_arrived(s):
        @pl.when(z <= NZ - 2)
        def _():
            if s == 1:
                first.wait_recv()
                dkv[ROW - TOK :, :] += first_in[...].astype(F32)
            else:
                ring[s - 2].wait_recv()
                dkv[...] += ring_in[s - 2].astype(F32)

    for s in range(1, WIN - 1):

        @pl.when(z >= WIN - 1 - s)
        def _():
            backward_row(s)
            add_arrived(s)
            ring_out[s - 1] = dkv[...].astype(BF16)
            ring[s - 1].start()

    backward_row(WIN - 1)

    def give(a, _):
        kept = keep[rows_of(a * TOK, TOK), :]
        value = acc_t[a] * SCALE
        for r in range(REP):
            piece = value[:, r * HD : (r + 1) * HD].T.astype(BF16)
            q_s[a, r * HD : (r + 1) * HD, :] = piece
            dq[a, :, r * HD : (r + 1) * HD] = (piece.astype(F32) * kept).astype(BF16)
        return 0

    lax.fori_loop(0, NX, give, 0)
    send_x(7)

    def z_pieces(peer):
        return [
            (scatq.at[rows_of(peer * 32, 32)], rxq.at[z]),
            (scatkv.at[rows_of(peer * 32, 32)], rxkv.at[z]),
            (vec_z, r_z.at[z]),
        ]

    own_z = [pltpu.make_async_copy(src, dst, own_sem.at[12 + k]) for k, (src, dst) in enumerate(z_pieces(z))]
    sent_z = []
    for d in range(1, NZ):
        peer = (z + d) % NZ
        sent_z.append([
            remote(src, dst, z_send.at[d - 1, k], z_recv.at[d - 1, k], ctx_of(peer, x))
            for k, (src, dst) in enumerate(z_pieces(peer))
        ])

    def send_z(k):
        for d in range(NZ - 1):
            sent_z[d][k].start()
        own_z[k].start()

    def arrived_z(k):
        own_z[k].wait()
        for d in range(NZ - 1):
            sent_z[d][k].wait_recv()

    vec[...] = jnp.zeros_like(vec)
    for r in range(REP):
        at = slice(r * HD, (r + 1) * HD)
        grads = jnp.concatenate([q_s[a, at, :] for a in range(NX)], axis=0)
        scattered = jnp.dot(onehot_t[...], grads, preferred_element_type=F32)
        scatq[:, at] = scattered.astype(BF16)
        vec[r : r + 1, :] = jnp.sum(scattered * raw[:, at].astype(F32), axis=0, keepdims=True)
        vec[10 + r : 11 + r, :] = jnp.sum(scattered, axis=0, keepdims=True)
    send_z(0)

    add_arrived(WIN - 1)
    whole[...] = dkv[...].astype(BF16)
    for k in range(2):
        at = slice(k * HD, (k + 1) * HD)
        mkv[:, at] = (whole[:, at].astype(F32) * keep[...]).astype(BF16)
    send_x(8)
    send_x(9)
    scattered = jnp.dot(onehot_t[...], whole[...], preferred_element_type=F32)
    scatkv[...] = scattered.astype(BF16)
    send_z(1)
    scale_part = jnp.sum(scattered * raw[:, QC:].astype(F32), axis=0, keepdims=True)
    shift_part = jnp.sum(scattered, axis=0, keepdims=True)
    for k in range(2):
        vec[REP + k : REP + k + 1, :] = scale_part[:, k * HD : (k + 1) * HD]
        vec[10 + REP + k : 11 + REP + k, :] = shift_part[:, k * HD : (k + 1) * HD]
    own_dp = pltpu.make_async_copy(vec, r_dp.at[dp], own_sem.at[15])
    sent_dp = [
        remote(vec, r_dp.at[dp], dp_send.at[d - 1], dp_recv.at[d - 1], {"dp": (dp + d) % NDP}) for d in range(1, NDP)
    ]
    for copy in sent_dp:
        copy.start()
    own_dp.start()

    own_dp.wait()
    for copy in sent_dp:
        copy.wait_recv()
    value = r_dp[0]
    for k in range(1, NDP):
        value = value + r_dp[k]
    vec_z[...] = value
    send_z(2)

    arrived_z(0)
    arrived_z(1)
    slots_q = rxq[0].astype(F32)
    slots_kv = rxkv[0].astype(F32)
    for k in range(1, NZ):
        slots_q = slots_q + rxq[k].astype(F32)
        slots_kv = slots_kv + rxkv[k].astype(F32)
    grad = jnp.concatenate([slots_q, slots_kv], axis=1) * proj[pl.ds(x, 1), :]
    for k in range(NX):
        piece = grad[k * SLOTS : (k + 1) * SLOTS]
        igs[k] = jnp.concatenate([piece[:, :HALF], piece[:, HALF:]], axis=0).astype(BF16)
    send_x(10)

    arrived_z(2)
    value = r_z[0]
    for k in range(1, NZ):
        value = value + r_z[k]
    vec_x[...] = value
    send_x(11)
    arrived_x(11)
    sums_out[...] = r_x[...]
    for k in range(6, 11):
        arrived_x(k)

    for k in range(4):

        @pl.when((z >= k) & (z <= NZ - 2))
        def _():
            passed(k).wait_send()

        @pl.when(z >= k + 1)
        def _():
            ring[3 - k].wait_send()

    @pl.when((z >= 4) & (z <= NZ - 2))
    def _():
        last.wait_send()

    @pl.when(z >= WIN - 1)
    def _():
        first.wait_send()

    for group in sent_x + sent_z + ups + downs:
        for copy in group:
            copy.wait_send()
    for copy in sent_dp:
        copy.wait_send()


def by_head(a):
    lead = a.shape[:-1]
    parts = [
        a[..., : NX * QC].reshape(*lead, NX, QC),
        a[..., NX * QC : NX * (QC + HD)].reshape(*lead, NX, HD),
        a[..., NX * (QC + HD) :].reshape(*lead, NX, HD),
    ]
    return jnp.concatenate(parts, axis=-1)


def from_heads(a):
    lead = a.shape[:-2]
    parts = [a[..., :QC], a[..., QC : QC + HD], a[..., QC + HD :]]
    return jnp.concatenate([part.reshape(*lead, -1) for part in parts], axis=-1)


def shape(dims, kind):
    return jax.ShapeDtypeStruct(dims, kind)


ANY = pl.BlockSpec(memory_space=pl.ANY)
VMEM = pl.BlockSpec(memory_space=pltpu.VMEM)
DMA = pltpu.SemaphoreType.DMA
LIMIT = 60 * 1024 * 1024


def per_device(
    text_rows, image_rows, tile_counts, tile_offsets, doc_ids, out_grad, proj_scale, proj_shift
):
    image = by_head(image_rows[0]).reshape(SLOTS, NX, 2, HALF)
    image = image.transpose(1, 2, 0, 3).reshape(NX, 16, HALF)
    slot = jnp.arange(TOK, dtype=jnp.int32)
    me = lax.axis_index("ctx")
    within = slot - SLOTS * (me % 16)
    live = (within >= 0) & (within < tile_counts[0, 0])
    target = jnp.where(live, tile_offsets[0, 0] + within + 1, 0)[None]
    row = jnp.arange(8, dtype=jnp.int32)[:, None]
    meta = jnp.where(row == 0, doc_ids, jnp.where(row == 1 + me // 16, target, 0))
    proj = jnp.concatenate([by_head(proj_scale), by_head(proj_shift)], axis=0)

    attn_out, text_grad, image_out, sums = pl.pallas_call(
        layer_kernel,
        out_shape=(
            shape((TOK, NX * QC), BF16),
            shape((TOK, NX * HC), BF16),
            shape((NX, 16, HALF), BF16),
            shape((NX, 24, HD), F32),
        ),
        in_specs=[ANY, ANY, ANY, ANY, VMEM],
        out_specs=(ANY, ANY, ANY, VMEM),
        scratch_shapes=[
            pltpu.VMEM((NX, TOK, QC), BF16),
            pltpu.VMEM((NX, TOK, QC), BF16),
            pltpu.VMEM((WIN, ROW, 2 * HD), BF16),
            pltpu.VMEM((NZ * NX, 16, HALF), BF16),
            pltpu.VMEM((NZ * NX, 8, TOK), jnp.int32),
            pltpu.VMEM((NSLOT, HC), BF16),
            pltpu.VMEM((NSLOT, HC), BF16),
            pltpu.VMEM((NSLOT, ROW), BF16),
            pltpu.VMEM((ROW, HD), F32),
            pltpu.VMEM((NX, 1, LANES), jnp.int32),
            pltpu.VMEM((NX, HD, LANES), BF16),
            pltpu.VMEM((NX, HD, LANES), BF16),
            pltpu.VMEM((NX, LANES, HD), BF16),
            pltpu.VMEM((NX, LANES, HD), BF16),
            pltpu.VMEM((WIN, ROW, HD), BF16),
            pltpu.VMEM((WIN, ROW, HD), BF16),
            pltpu.VMEM((WIN, HD, ROW), BF16),
            pltpu.VMEM((WIN, HD, ROW), BF16),
            pltpu.VMEM((WIN - 1, NX, ROW, LANES), BF16),
            pltpu.VMEM((TOK, LANES), BF16),
            pltpu.VMEM((NX, HD, LANES), F32),
            pltpu.VMEM((NX, 1, LANES), F32),
            pltpu.VMEM((NX, 1, LANES), F32),
            pltpu.VMEM((WIN, NX, 1, LANES), F32),
            pltpu.VMEM((NX, 1, LANES), F32),
            pltpu.VMEM((ROW, 2 * HD), F32),
            pltpu.VMEM((NX, TOK, QC), BF16),
            pltpu.VMEM((NX, TOK, QC), BF16),
            pltpu.VMEM((TOK, 2 * HD), BF16),
            pltpu.VMEM((TOK, 2 * HD), BF16),
            pltpu.VMEM((4, ROW, 2 * HD), BF16),
            pltpu.VMEM((4, ROW, 2 * HD), BF16),
            pltpu.VMEM((ROW, 2 * HD), BF16),
            pltpu.VMEM((ROW, 2 * HD), BF16),
            pltpu.VMEM((NSLOT, QC), BF16),
            pltpu.VMEM((NSLOT, 2 * HD), BF16),
            pltpu.VMEM((NZ, 32, QC), BF16),
            pltpu.VMEM((NZ, 32, 2 * HD), BF16),
            pltpu.VMEM((NX, 16, HALF), BF16),
            pltpu.VMEM((24, HD), F32),
            pltpu.VMEM((24, HD), F32),
            pltpu.VMEM((24, HD), F32),
            pltpu.VMEM((NDP, 24, HD), F32),
            pltpu.VMEM((NZ, 24, HD), F32),
            pltpu.VMEM((NX, 24, HD), F32),
            DMA((16,)), DMA((3, 12)), DMA((3, 12)), DMA((5,)), DMA((5,)),
            DMA((3, 2)), DMA((3, 2)), DMA((4, 2)), DMA((4, 2)),
            DMA((5,)), DMA((5,)), DMA((7, 3)), DMA((7, 3)), DMA((7,)), DMA((7,)),
        ],
        compiler_params=pltpu.CompilerParams(
            collective_id=0, has_side_effects=True, vmem_limit_bytes=LIMIT
        ),
        name="layer",
    )(text_rows[0], out_grad[0], image, meta, proj)

    image_grad = image_out.reshape(NX, 2, SLOTS, HALF).transpose(2, 0, 1, 3).reshape(SLOTS, NX, HC)
    image_grad = from_heads(image_grad)[None]
    scale_grad = from_heads(sums[:, :10].reshape(NX, HC))
    shift_grad = from_heads(sums[:, 10:20].reshape(NX, HC))
    return (attn_out[None], text_grad[None], image_grad, scale_grad, shift_grad)


def solution(mesh):
    return jax.shard_map(
        per_device,
        mesh=mesh,
        in_specs=(
            P("dp", "ctx", None),
            P("dp", "ctx", None),
            P("dp", "ctx"),
            P("dp", "ctx"),
            P("dp", "ctx"),
            P("dp", "ctx", None),
            P(),
            P(),
        ),
        out_specs=(P("dp", "ctx", None), P("dp", "ctx", None), P("dp", "ctx", None), P(), P()),
        check_vma=False,
    )
```

time: 893 us -> 144 us (0.16)
  waiting for transfers between devices: 692 us -> 0 us
  Pallas kernels: 0 us -> 126 us
  blocking collectives: 97.4 us -> 0 us
  local copies, waits for them, and re-layouts: 50.5 us -> 9.59 us
  matrix products: 17 us -> 0 us
  between operations: 15.3 us -> 2.03 us
  other arithmetic: 16.3 us -> 4.47 us
    unnamed x5 -> x0, waiting for transfers between devices: 332 us -> none
    reduce_scatter x1 -> x0, waiting for transfers between devices: 212 us -> none  [per_device(): lax.psum_scatter(scattered.astype(jnp.bfloat16), 'ctx', scatter_dimension...]
    all_gather x2 -> x0, waiting for transfers between devices: 148 us -> none  [the longest x1 90.6 us: per_device(): lax.all_gather(keyval, 'ctx', axis=0, tiled=True)]
    pallas_call x0 -> x1, Pallas kernels: none -> 126 us  [per_device(): pl.pallas_call(layer_kernel, out_shape=(shape((TOK, NX * QC), BF16), shap...]
    psum x2 -> x0, blocking collectives: 97.4 us -> none  [the longest x1 74 us: per_device(): scale_grad, shift_grad = lax.psum((scale_part, shift_part), ('dp', 'ctx'))]
    unnamed x27 -> x11, local copies, waits for them, and re-layouts: 31.6 us -> 4.23 us
    dot_general x8 -> x0, matrix products: 17 us -> none  [the longest x1 3.09 us: backward_step(): jnp.einsum('pgrd,tgd->grpt', dout, vals, preferred_element_type=jnp.float32)]
  transfers between devices with their start and end apart: 4 -> 0, of which waited for: 4 -> 0; matrix products, arithmetic and copies ran while one was open for 1% -> 0% of each run, Pallas kernels for 0% -> 0%
where the time goes in v2:
time: 144 us; the launch traced here: 142 us
  Pallas kernels  126 us (88%)
  local copies, waits for them, and re-layouts  9.59 us (7%)
  other arithmetic  4.47 us (3%)
  between operations  2.03 us (1%)
    pallas_call x1, Pallas kernels, per_device(): pl.pallas_call(layer_kernel, out_shape=(shape((TOK, NX * QC), BF16), shap...  126 us
    unnamed x11, local copies, waits for them, and re-layouts  4.23 us

profile of v2, /device:TPU:8, one launch (start us, length us, event | category | flops | bytes accessed | tf_op | source)
XLA Modules:
  0.0 142.1 jit_solution(821817127253544810)
XLA Ops:
  2.0 1.3 select_select_fusion.meta
  3.3 0.8 slice_bitcast_fusion.13
  4.1 0.7 slice.123
  4.8 0.7 slice.129
  5.5 0.6 maximum_maximum_fusion.proj
  6.2 0.7 slice_bitcast_fusion.7
  6.9 0.8 slice.146
  7.7 0.6 pad_maximum_fusion
  8.4 126.0 %layer.1 = (bf16[128,4096]{1,0:T(8,128)(2,1)}, bf16[128,5120]{1,0:T(8,128)(2,1)}, bf16[4,16,640]{2,1,0:T(8,128)(2,1)}, f32[4,24,128]{2,1,0:T(8,128)}) custom-call(bf16[128,5120]{1,0:T(8,128)(2,1)} %bitcast.68, bf16[128,4096]{1,0:T(8,128)(2,1)} %bitcast.70, bf16[4,16,640]{2,1,0:T(8,128)(2,1)} %bitcast.72, s32[8,128]{1,0:T(8,128)} %select_select_fusion.meta, ...), custom_call_target="tpu_custom_call" | custom-call | tf_op jit(solution)/shard_map/layer/pallas_call | solution.py:535
  134.4 0.8 slice_bitcast_fusion
  135.2 0.6 pad_maximum_fusion.2
  135.9 0.0 copy-start
  135.9 0.6 pad_maximum_fusion.1
  136.5 0.8 slice.149
  137.4 0.7 slice_bitcast_fusion.5
  138.1 0.6 maximum_bitcast_fusion
  138.7 2.3 %copy.29 = bf16[1,128,4096]{2,1,0:T(8,128)(2,1)} copy(bf16[1,128,4096]{2,1,0:T(8,128)(2,1)} %bitcast.71) | data formatting | bytes 2097152
  141.0 0.0 copy-done
  141.0 1.1 copy.30
  (12 shorter events, 0.1 us)
Async XLA Ops:
  135.9 5.2 %copy-start = (bf16[128,5120]{1,0:T(8,128)(2,1)S(1)}, bf16[128,5120]{1,0:T(8,128)(2,1)}, u32[]{:S(2)}) copy-start(bf16[128,5120]{1,0:T(8,128)(2,1)} %get-tuple-element.10) | copy-start | bytes 3932164

commit v3 on v2

--- a/solution.py
+++ b/solution.py
@@ -60,23 +60,42 @@
 
 
 def layer_kernel(
-    text, dout, image, meta, proj,
-    attn_out, text_grad, image_out, sums_out,
-    q_in, do_in, kvw, images, metas, raw, adapted, onehot_t, keep, starts,
+    text, dout, image_rows, counts, offsets, doc_ids, proj_scale, proj_shift,
+    attn_out, text_grad, image_grad, scale_out, shift_out,
+    image, meta, image_out, q_in, do_in, kvw, images, metas, raw, adapted, onehot_t, keep,
     q_t, do_t, q_s, do_s, ks, vs, kts, vts, p_buf, p_first, acc_t, top, total, tops, corr, dkv,
     attn, dq, first_in, first_out, ring_in, ring_out, whole, mkv, scatq, scatkv, rxq, rxkv, igs,
     vec, vec_z, vec_x, r_dp, r_z, r_x,
-    own_sem, x_send, x_recv, kv_send, kv_recv, up_send, up_recv, down_send, down_recv,
+    img_send, img_recv, key_send, key_recv, own_sem, x_send, x_recv, kv_send, kv_recv, up_send, up_recv, down_send, down_recv,
     ring_send, ring_recv, z_send, z_recv, dp_send, dp_recv,
 ):
     dp, z, x = place()
     up, down = (z + 1) % NZ, (z + NZ - 1) % NZ
     me = z * NX + x
     base = z * ROW
+
+    def of_head(ref, head):
+        parts = [ref[pl.ds(head * REP + r, 1), :] for r in range(REP)]
+        parts += [ref[pl.ds(NX * REP + head, 1), :], ref[pl.ds(NX * (REP + 1) + head, 1), :]]
+        return jnp.concatenate(parts, axis=1)
+
+    for head in range(NX):
+        key, val = NX * QC + head * HD, NX * (QC + HD) + head * HD
+        both = jnp.concatenate(
+            [image_rows[:, head * QC : (head + 1) * QC], image_rows[:, key : key + HD], image_rows[:, val : val + HD]],
+            axis=1,
+        ).astype(F32)
+        image[head] = jnp.concatenate([both[:, :HALF], both[:, HALF:]], axis=0).astype(BF16)
+    lane = lax.broadcasted_iota(jnp.int32, (8, TOK), 1) - SLOTS * (me % 16)
+    row = lax.broadcasted_iota(jnp.int32, (8, TOK), 0)
+    live = (lane >= 0) & (lane < counts[...])
+    filled = jnp.where(live, offsets[...] + lane + 1, 0)
+    meta[...] = jnp.where(row == 0, doc_ids[...], jnp.where(row == 1 + me // 16, filled, 0))
     greet(
         [ctx_of(z, (x + d) % NX) for d in range(1, NX)]
         + [ctx_of((z + d) % NZ, x) for d in range(1, NZ)]
         + [{"dp": (dp + d) % NDP} for d in range(1, NDP)]
+        + [ctx_of(near, (x + d) % NX) for near in (up, down) for d in range(1, NX)]
     )
 
     def pieces(peer):
@@ -115,55 +134,107 @@
         for d in range(NX - 1):
             sent_x[d][k].wait_recv()
 
-    for k in range(6):
-        send_x(k)
-
-    ups, downs = [], []
-    for k in range(3):
+    def image_step(near, way, d, k):
+        head = (x + d) % NX
+        src, dst = pieces(head)[k]
+        return remote(src, dst, img_send.at[way, d, k], img_recv.at[way, x, k], ctx_of(near, head))
+
+    def image_came(near, way, j, k):
+        src, dst = pieces(j)[k]
+        return remote(src, dst, img_send.at[way, 0, k], img_recv.at[way, j, k], ctx_of(near, j))
+
+    def key_step(d, k):
+        head = (x + d) % NX
+        at = kvw.at[WIN - 2, rows_of(x * TOK, TOK), pl.ds(k * HD, HD)]
+        src = text.at[:, cols(NX * QC + (NX * k + head) * HD, HD)]
+        return remote(src, at, key_send.at[d, k], key_recv.at[x, k], ctx_of(up, head))
+
+    def key_came(j, k):
+        at = kvw.at[WIN - 2, rows_of(j * TOK, TOK), pl.ds(k * HD, HD)]
+        src = text.at[:, cols(NX * QC + NX * k * HD, HD)]
+        return remote(src, at, key_send.at[0, k], key_recv.at[j, k], ctx_of(up, x))
+
+    send_x(0)
+    send_x(1)
+    for k in range(2):
+        for d in range(NX):
+            image_step(up, 0, d, k).start()
+            image_step(down, 1, d, k).start()
+    send_x(2)
+    send_x(3)
+
+    @pl.when(z <= NZ - 2)
+    def _():
+        for d in range(NX):
+            for k in range(2):
+                key_step(d, k).start()
+
+    send_x(4)
+    send_x(5)
+
+    ups, downs = [None], [None]
+    for k in range(1, 3):
         block = pl.ds(((z + NZ - k) % NZ) * NX, NX)
         ups.append([
             remote(a.at[block], a.at[block], up_send.at[k, j], up_recv.at[k, j], ctx_of(up, x))
             for j, a in enumerate((metas, images))
         ])
-    for k in range(4):
+    for k in range(1, 4):
         block = pl.ds(((z + k) % NZ) * NX, NX)
         downs.append([
             remote(a.at[block], a.at[block], down_send.at[k, j], down_recv.at[k, j], ctx_of(down, x))
             for j, a in enumerate((metas, images))
         ])
 
-    def passed(k):
+    def hop(k, j):
+        part = rows_of(j * TOK, TOK)
         return remote(
-            kvw.at[WIN - 1 - k], kvw.at[WIN - 2 - k], kv_send.at[k], kv_recv.at[k], ctx_of(up, x)
+            kvw.at[WIN - 1 - k, part], kvw.at[WIN - 2 - k, part], kv_send.at[k, j], kv_recv.at[k, j], ctx_of(up, x)
         )
 
-    tail = pl.ds(ROW - TOK, TOK)
-    last = remote(kvw.at[1, tail], kvw.at[0, tail], kv_send.at[4], kv_recv.at[4], ctx_of(up, x))
-
-    arrived_x(0)
-    arrived_x(1)
-    for j in range(2):
-        ups[0][j].start()
-        downs[0][j].start()
-    arrived_x(2)
-    arrived_x(3)
-
-    @pl.when(z <= NZ - 2)
-    def _():
-        passed(0).start()
-
-    for k in range(1, 5):
+    def pass_keys(k, j):
+        @pl.when(z >= k)
+        def _():
+            if k == 1:
+                key_came(j, 0).wait_recv()
+                key_came(j, 1).wait_recv()
+            else:
+                hop(k - 1, j).wait_recv()
+
+        @pl.when((z >= k) & (z <= NZ - 2) & ((k < 4) | (j == NX - 1)))
+        def _():
+            hop(k, j).start()
+
+    def pass_images(k):
         for j in range(2):
-            if k <= 3:
+            if k == 1:
+                for d in range(NX):
+                    image_came(up, 0, d, j).wait_recv()
+            elif k <= 3:
                 ups[k - 1][j].wait_recv()
             if k < 3:
                 ups[k][j].start()
-            downs[k - 1][j].wait_recv()
+            if k == 1:
+                for d in range(NX):
+                    image_came(down, 1, d, j).wait_recv()
+            else:
+                downs[k - 1][j].wait_recv()
             if k < 4:
                 downs[k][j].start()
 
-    scale = proj[pl.ds(x, 1), :]
-    shift = proj[pl.ds(NX + x, 1), :]
+    pass_images(1)
+    for j in range(NX):
+        pass_keys(1, j)
+    pass_images(2)
+    for j in range(NX):
+        pass_keys(2, j)
+    pass_images(3)
+    for k in range(4):
+        arrived_x(k)
+    pass_images(4)
+
+    scale = of_head(proj_scale, x)
+    shift = of_head(proj_shift, x)
 
     def adapt(pair, _):
         first = images[2 * pair].astype(F32)
@@ -180,12 +251,6 @@
     lax.fori_loop(0, NSLOT // 16, adapt, 0)
     all_metas = jnp.sum(metas[:, 1:3, :], axis=0)
     target = jnp.concatenate([all_metas[0:1], all_metas[1:2]], axis=1) - 1
-    all_docs = metas[:, 0, :]
-    before = [
-        jnp.sum(jnp.where(all_docs < doc, 1, 0).astype(F32), axis=(0, 1), keepdims=True).astype(jnp.int32)
-        for doc in range(1, DOCS)
-    ]
-
     def chosen(begin, size):
         position = begin + lax.broadcasted_iota(jnp.int32, (size, NSLOT), 0)
         hit = jnp.where(position == target, 1.0, 0.0).astype(F32)
@@ -202,12 +267,10 @@
         for r in range(REP):
             piece = value[:, r * HD : (r + 1) * HD]
             q_s[a, r * HD : (r + 1) * HD, :] = piece.astype(BF16)
-            q_t[a, :, r * HD : (r + 1) * HD] = piece.T.astype(BF16)
-        docs = metas[z * NX + a, 0:1, :]
-        start = jnp.zeros((1, TOK), jnp.int32)
-        for doc in range(1, DOCS):
-            start = jnp.where(docs == doc, before[doc - 1], start)
-        starts[a] = jnp.concatenate([start] * REP, axis=1)
+            q_t[a, :HD, r * HD : (r + 1) * HD] = piece.T.astype(BF16)
+        docs = jnp.concatenate([metas[z * NX + a, 0:1, :]] * REP, axis=1)
+        other = lax.broadcasted_iota(jnp.int32, (HD, LANES), 0) != docs
+        q_t[a, HD:, :] = jnp.where(other, -1e30, 0.0).astype(BF16)
         top[a] = jnp.full((1, LANES), -1e30, F32)
         total[a] = jnp.zeros((1, LANES), F32)
         acc_t[a] = jnp.zeros((HD, LANES), F32)
@@ -219,7 +282,10 @@
         hit, is_image = chosen(base + (s - (WIN - 1)) * ROW + at, size)
         picked = jnp.dot(hit.astype(BF16), adapted[:, QC:], preferred_element_type=F32)
         both = jnp.where(is_image > 0.0, picked, kvw[s, at : at + size].astype(F32))
-        ks[s, at : at + size, :] = both[:, :HD].astype(BF16)
+        ks[s, at : at + size, :HD] = both[:, :HD].astype(BF16)
+        for j in range(at // TOK, (at + size) // TOK):
+            same = lax.broadcasted_iota(jnp.int32, (HD, TOK), 0) == metas[(z + s - (WIN - 1)) * NX + j, 0:1, :]
+            ks[s, j * TOK : (j + 1) * TOK, HD:] = jnp.where(same, 1.0, 0.0).astype(F32).T.astype(BF16)
         vs[s, at : at + size, :] = both[:, HD:].astype(BF16)
         kts[s, :, at : at + size] = both[:, :HD].T.astype(BF16)
         vts[s, :, at : at + size] = both[:, HD:].T.astype(BF16)
@@ -227,63 +293,81 @@
     within = lax.broadcasted_iota(jnp.int32, (1, TOK), 1)
     within = jnp.concatenate([within] * REP, axis=1)
 
-    def forward(s, a, at, size, keep_prob):
-        key_pos = base + (s - (WIN - 1)) * ROW + at + lax.broadcasted_iota(jnp.int32, (size, 1), 0)
-        value = jnp.dot(ks[s, at : at + size, :], q_t[a], preferred_element_type=F32) * (SCALE * LOG2E)
-        value = jnp.where((key_pos >= starts[a]) & (key_pos <= base + a * TOK + within), value, -1e30)
+    def forward(s, a, at, size, keep_prob, diagonal):
+        value = jnp.dot(ks[s, at : at + size, :], q_t[a], preferred_element_type=F32)
+        if diagonal:
+            key_at = at + lax.broadcasted_iota(jnp.int32, (size, 1), 0)
+            value = jnp.where(key_at <= a * TOK + within, value, -1e30)
         old = top[a]
         new = jnp.maximum(old, jnp.max(value, axis=0, keepdims=True))
         top[a] = new
         tops[s, a] = new
-        factor = jnp.exp2(old - new)
-        prob = jnp.exp2(value - new)
+        factor = jnp.exp2((old - new) * (SCALE * LOG2E))
+        prob = jnp.exp2((value - new) * (SCALE * LOG2E))
         total[a] = total[a] * factor + jnp.sum(prob, axis=0, keepdims=True)
         prob_b = prob.astype(BF16)
         keep_prob(prob_b)
         acc_t[a] = acc_t[a] * factor + jnp.dot(vts[s, :, at : at + size], prob_b, preferred_element_type=F32)
 
+    place_keys(WIN - 1, 0, ROW)
+
+    def forward_own(a, _):
+        pass_keys(3, a)
+
+        def keep_prob(prob):
+            p_buf[WIN - 2, a] = prob
+
+        forward(WIN - 1, a, 0, ROW, keep_prob, True)
+        return 0
+
+    lax.fori_loop(0, NX, forward_own, 0)
+
     def forward_row(k, _):
         s = WIN - 1 - k
-
-        @pl.when(k >= 1)
-        def _():
-            passed(k - 1).wait_recv()
-
-        @pl.when((k >= 1) & (k <= 3) & (z <= NZ - 2))
-        def _():
-            passed(k).start()
-
-        @pl.when((k == 4) & (z <= NZ - 2))
-        def _():
-            last.start()
-
         place_keys(s, 0, ROW)
 
         def one(a, _):
+            @pl.when(k == 1)
+            def _():
+                pass_keys(4, a)
+
             def keep_prob(prob):
                 p_buf[s - 1, a] = prob
 
-            forward(s, a, 0, ROW, keep_prob)
+            forward(s, a, 0, ROW, keep_prob, False)
             return 0
 
         lax.fori_loop(0, NX, one, 0)
         return 0
 
-    lax.fori_loop(0, jnp.minimum(z + 1, 5), forward_row, 0)
+    lax.fori_loop(1, jnp.minimum(z + 1, 5), forward_row, 0)
 
     @pl.when(z >= WIN - 1)
     def _():
-        last.wait_recv()
+        hop(4, NX - 1).wait_recv()
         place_keys(0, ROW - TOK, TOK)
 
         def keep_prob(prob):
             p_first[...] = prob
 
-        forward(0, 0, ROW - TOK, TOK, keep_prob)
+        forward(0, 0, ROW - TOK, TOK, keep_prob, False)
 
     arrived_x(5)
 
-    def finish(a, _):
+    def send_turn(i, k, src, columns):
+        peer = (x + i + 1) % NX
+
+        @pl.when(i < NX - 1)
+        def _():
+            at = jnp.minimum(i, NX - 2)
+            remote(src.at[peer], columns, x_send.at[at, k], x_recv.at[at, k], ctx_of(z, peer)).start()
+
+        @pl.when(i == NX - 1)
+        def _():
+            own_x[k].start()
+
+    def finish(i, _):
+        a = (x + i + 1) % NX
         for r in range(REP):
             piece = do_in[a, :, r * HD : (r + 1) * HD]
             do_s[a, r * HD : (r + 1) * HD, :] = piece
@@ -295,13 +379,13 @@
         for r in range(REP):
             attn[a, :, r * HD : (r + 1) * HD] = out_t[:, r * HD : (r + 1) * HD].T.astype(BF16)
         acc_t[a] = jnp.zeros((HD, LANES), F32)
+        send_turn(i, 6, attn, attn_out.at[:, cols(x * QC, QC)])
         return 0
 
     lax.fori_loop(0, NX, finish, 0)
-    send_x(6)
 
     def backward(s, a, at, size, prob_b):
-        part = jnp.exp2(tops[s, a] - top[a]) * total[a]
+        part = jnp.exp2((tops[s, a] - top[a]) * (SCALE * LOG2E)) * total[a]
         prob = prob_b.astype(F32) * part
         dprob = jnp.dot(vs[s, at : at + size, :], do_t[a], preferred_element_type=F32)
         dscore = (prob * (dprob - corr[a])).astype(BF16)
@@ -310,11 +394,12 @@
         dv = jnp.dot(prob.astype(BF16), do_s[a], preferred_element_type=F32)
         return dk, dv
 
-    first = remote(first_out, first_in, ring_send.at[0], ring_recv.at[0], ctx_of(down, x))
-    ring = [
-        remote(ring_out.at[k], ring_in.at[k], ring_send.at[1 + k], ring_recv.at[1 + k], ctx_of(down, x))
-        for k in range(4)
-    ]
+    first = remote(first_out, first_in, ring_send.at[0, 0], ring_recv.at[0, 0], ctx_of(down, x))
+    def ring(k, j):
+        part = rows_of(j * TOK, TOK)
+        return remote(
+            ring_out.at[k, part], ring_in.at[k, part], ring_send.at[1 + k, j], ring_recv.at[1 + k, j], ctx_of(down, x)
+        )
 
     @pl.when(z >= WIN - 1)
     def _():
@@ -323,57 +408,66 @@
         first_out[:, HD:] = dv.astype(BF16)
         first.start()
 
-    def backward_row(s):
-        def one(a, _):
-            dk, dv = backward(s, a, 0, ROW, p_buf[s - 1, a])
-
-            @pl.when(a == 0)
-            def _():
-                dkv[:, :HD] = dk
-                dkv[:, HD:] = dv
-
-            @pl.when(a > 0)
-            def _():
-                dkv[:, :HD] += dk
-                dkv[:, HD:] += dv
-
-            return 0
-
-        lax.fori_loop(0, NX, one, 0)
-        dkv[:, :HD] = dkv[:, :HD] * SCALE
-
-    def add_arrived(s):
-        @pl.when(z <= NZ - 2)
+    def backward_tile(s, a, begin):
+        dk, dv = backward(s, a, 0, ROW, p_buf[s - 1, a])
+
+        @pl.when(begin)
+        def _():
+            dkv[:, :HD] = dk
+            dkv[:, HD:] = dv
+
+        @pl.when(jnp.logical_not(begin))
+        def _():
+            dkv[:, :HD] += dk
+            dkv[:, HD:] += dv
+
+    def summed(s, j):
+        part = rows_of(j * TOK, TOK)
+        whole[part, :HD] = (dkv[part, :HD] * SCALE).astype(BF16)
+        whole[part, HD:] = dkv[part, HD:].astype(BF16)
+
+        def add(arrived):
+            whole[part, :HD] = (dkv[part, :HD] * SCALE + arrived[:, :HD].astype(F32)).astype(BF16)
+            whole[part, HD:] = (dkv[part, HD:] + arrived[:, HD:].astype(F32)).astype(BF16)
+
+        @pl.when((z <= NZ - 2) & ((s >= 2) | (j == NX - 1)))
         def _():
             if s == 1:
                 first.wait_recv()
-                dkv[ROW - TOK :, :] += first_in[...].astype(F32)
+                add(first_in[...])
             else:
-                ring[s - 2].wait_recv()
-                dkv[...] += ring_in[s - 2].astype(F32)
+                ring(s - 2, j).wait_recv()
+                add(ring_in[s - 2, part, :])
+
+        return part
 
     for s in range(1, WIN - 1):
 
         @pl.when(z >= WIN - 1 - s)
         def _():
-            backward_row(s)
-            add_arrived(s)
-            ring_out[s - 1] = dkv[...].astype(BF16)
-            ring[s - 1].start()
-
-    backward_row(WIN - 1)
-
-    def give(a, _):
+            def one(a, _):
+                backward_tile(s, a, a == 0)
+                return 0
+
+            lax.fori_loop(0, NX, one, 0)
+            for j in range(NX):
+                part = summed(s, j)
+                ring_out[s - 1, part, :] = whole[part, :]
+                ring(s - 1, j).start()
+
+    def end(i, _):
+        a = (x + i + 1) % NX
+        backward_tile(WIN - 1, a, i == 0)
         kept = keep[rows_of(a * TOK, TOK), :]
         value = acc_t[a] * SCALE
         for r in range(REP):
             piece = value[:, r * HD : (r + 1) * HD].T.astype(BF16)
             q_s[a, r * HD : (r + 1) * HD, :] = piece
             dq[a, :, r * HD : (r + 1) * HD] = (piece.astype(F32) * kept).astype(BF16)
+        send_turn(i, 7, dq, text_grad.at[:, cols(x * QC, QC)])
         return 0
 
-    lax.fori_loop(0, NX, give, 0)
-    send_x(7)
+    lax.fori_loop(0, NX, end, 0)
 
     def z_pieces(peer):
         return [
@@ -411,13 +505,17 @@
         vec[10 + r : 11 + r, :] = jnp.sum(scattered, axis=0, keepdims=True)
     send_z(0)
 
-    add_arrived(WIN - 1)
-    whole[...] = dkv[...].astype(BF16)
-    for k in range(2):
-        at = slice(k * HD, (k + 1) * HD)
-        mkv[:, at] = (whole[:, at].astype(F32) * keep[...]).astype(BF16)
-    send_x(8)
-    send_x(9)
+    for i in range(NX):
+        j = (x + i + 1) % NX
+        part = summed(WIN - 1, j)
+        kept = keep[part, :]
+        mkv[part, :HD] = (whole[part, :HD].astype(F32) * kept).astype(BF16)
+        mkv[part, HD:] = (whole[part, HD:].astype(F32) * kept).astype(BF16)
+        for k in (8, 9):
+            if i < NX - 1:
+                sent_x[i][k].start()
+            else:
+                own_x[k].start()
     scattered = jnp.dot(onehot_t[...], whole[...], preferred_element_type=F32)
     scatkv[...] = scattered.astype(BF16)
     send_z(1)
@@ -450,7 +548,7 @@
     for k in range(1, NZ):
         slots_q = slots_q + rxq[k].astype(F32)
         slots_kv = slots_kv + rxkv[k].astype(F32)
-    grad = jnp.concatenate([slots_q, slots_kv], axis=1) * proj[pl.ds(x, 1), :]
+    grad = jnp.concatenate([slots_q, slots_kv], axis=1) * scale
     for k in range(NX):
         piece = grad[k * SLOTS : (k + 1) * SLOTS]
         igs[k] = jnp.concatenate([piece[:, :HALF], piece[:, HALF:]], axis=0).astype(BF16)
@@ -463,49 +561,65 @@
     vec_x[...] = value
     send_x(11)
     arrived_x(11)
-    sums_out[...] = r_x[...]
-    for k in range(6, 11):
+    for head in range(NX):
+        for out, at in ((scale_out, 0), (shift_out, 10)):
+            out[head * REP : (head + 1) * REP, :] = r_x[head, at : at + REP, :]
+            out[NX * REP + head : NX * REP + head + 1, :] = r_x[head, at + REP : at + REP + 1, :]
+            out[NX * (REP + 1) + head : NX * (REP + 1) + head + 1, :] = r_x[head, at + REP + 1 : at + REP + 2, :]
+    arrived_x(10)
+    for head in range(NX):
+        key, val = NX * QC + head * HD, NX * (QC + HD) + head * HD
+        both = image_out[head].astype(F32)
+        both = jnp.concatenate([both[:SLOTS], both[SLOTS:]], axis=1).astype(BF16)
+        image_grad[:, head * QC : (head + 1) * QC] = both[:, :QC]
+        image_grad[:, key : key + HD] = both[:, QC : QC + HD]
+        image_grad[:, val : val + HD] = both[:, QC + HD :]
+    for k in range(6, 10):
         arrived_x(k)
 
     for k in range(4):
 
         @pl.when((z >= k) & (z <= NZ - 2))
         def _():
-            passed(k).wait_send()
+            for j in range(NX):
+                if k == 0:
+                    key_step(j, 0).wait_send()
+                    key_step(j, 1).wait_send()
+                else:
+                    hop(k, j).wait_send()
 
         @pl.when(z >= k + 1)
         def _():
-            ring[3 - k].wait_send()
+            for j in range(NX):
+                ring(3 - k, j).wait_send()
 
     @pl.when((z >= 4) & (z <= NZ - 2))
     def _():
-        last.wait_send()
+        hop(4, NX - 1).wait_send()
 
     @pl.when(z >= WIN - 1)
     def _():
         first.wait_send()
 
-    for group in sent_x + sent_z + ups + downs:
+    for k in range(2):
+        for d in range(NX):
+            image_step(up, 0, d, k).wait_send()
+            image_step(down, 1, d, k).wait_send()
+    for group in sent_x + sent_z + ups[1:] + downs[1:]:
         for copy in group:
             copy.wait_send()
     for copy in sent_dp:
         copy.wait_send()
 
 
-def by_head(a):
-    lead = a.shape[:-1]
-    parts = [
-        a[..., : NX * QC].reshape(*lead, NX, QC),
-        a[..., NX * QC : NX * (QC + HD)].reshape(*lead, NX, HD),
-        a[..., NX * (QC + HD) :].reshape(*lead, NX, HD),
-    ]
-    return jnp.concatenate(parts, axis=-1)
-
-
-def from_heads(a):
-    lead = a.shape[:-2]
-    parts = [a[..., :QC], a[..., QC : QC + HD], a[..., QC + HD :]]
-    return jnp.concatenate([part.reshape(*lead, -1) for part in parts], axis=-1)
+def land_kernel(*refs):
+    half = len(refs) // 2
+    sems = refs[-1]
+    copies = [pltpu.make_async_copy(refs[k], refs[half + k], sems.at[k]) for k in range(half)]
+    for copy in copies:
+        copy.start()
+    for copy in copies:
+        copy.wait()
 
 
 def shape(dims, kind):
@@ -521,28 +635,21 @@
 def per_device(
     text_rows, image_rows, tile_counts, tile_offsets, doc_ids, out_grad, proj_scale, proj_shift
 ):
-    image = by_head(image_rows[0]).reshape(SLOTS, NX, 2, HALF)
-    image = image.transpose(1, 2, 0, 3).reshape(NX, 16, HALF)
-    slot = jnp.arange(TOK, dtype=jnp.int32)
-    me = lax.axis_index("ctx")
-    within = slot - SLOTS * (me % 16)
-    live = (within >= 0) & (within < tile_counts[0, 0])
-    target = jnp.where(live, tile_offsets[0, 0] + within + 1, 0)[None]
-    row = jnp.arange(8, dtype=jnp.int32)[:, None]
-    meta = jnp.where(row == 0, doc_ids, jnp.where(row == 1 + me // 16, target, 0))
-    proj = jnp.concatenate([by_head(proj_scale), by_head(proj_shift)], axis=0)
-
-    attn_out, text_grad, image_out, sums = pl.pallas_call(
+    attn_out, text_grad, image_grad, scale_grad, shift_grad = pl.pallas_call(
         layer_kernel,
         out_shape=(
             shape((TOK, NX * QC), BF16),
             shape((TOK, NX * HC), BF16),
-            shape((NX, 16, HALF), BF16),
-            shape((NX, 24, HD), F32),
+            shape((SLOTS, NX * HC), BF16),
+            shape((NX * HC // HD, HD), F32),
+            shape((NX * HC // HD, HD), F32),
         ),
-        in_specs=[ANY, ANY, ANY, ANY, VMEM],
-        out_specs=(ANY, ANY, ANY, VMEM),
+        in_specs=[ANY, ANY] + [VMEM] * 6,
+        out_specs=(ANY, ANY, VMEM, VMEM, VMEM),
         scratch_shapes=[
+            pltpu.VMEM((NX, 16, HALF), BF16),
+            pltpu.VMEM((8, TOK), jnp.int32),
+            pltpu.VMEM((NX, 16, HALF), BF16),
             pltpu.VMEM((NX, TOK, QC), BF16),
             pltpu.VMEM((NX, TOK, QC), BF16),
             pltpu.VMEM((WIN, ROW, 2 * HD), BF16),
@@ -552,12 +659,11 @@
             pltpu.VMEM((NSLOT, HC), BF16),
             pltpu.VMEM((NSLOT, ROW), BF16),
             pltpu.VMEM((ROW, HD), F32),
-            pltpu.VMEM((NX, 1, LANES), jnp.int32),
-            pltpu.VMEM((NX, HD, LANES), BF16),
+            pltpu.VMEM((NX, 2 * HD, LANES), BF16),
             pltpu.VMEM((NX, HD, LANES), BF16),
             pltpu.VMEM((NX, LANES, HD), BF16),
             pltpu.VMEM((NX, LANES, HD), BF16),
-            pltpu.VMEM((WIN, ROW, HD), BF16),
+            pltpu.VMEM((WIN, ROW, 2 * HD), BF16),
             pltpu.VMEM((WIN, ROW, HD), BF16),
             pltpu.VMEM((WIN, HD, ROW), BF16),
             pltpu.VMEM((WIN, HD, ROW), BF16),
@@ -588,21 +694,32 @@
             pltpu.VMEM((NDP, 24, HD), F32),
             pltpu.VMEM((NZ, 24, HD), F32),
             pltpu.VMEM((NX, 24, HD), F32),
-            DMA((16,)), DMA((3, 12)), DMA((3, 12)), DMA((5,)), DMA((5,)),
+            DMA((2, 4, 2)), DMA((2, 4, 2)), DMA((4, 2)), DMA((4, 2)),
+            DMA((16,)), DMA((3, 12)), DMA((3, 12)), DMA((5, 4)), DMA((5, 4)),
             DMA((3, 2)), DMA((3, 2)), DMA((4, 2)), DMA((4, 2)),
-            DMA((5,)), DMA((5,)), DMA((7, 3)), DMA((7, 3)), DMA((7,)), DMA((7,)),
+            DMA((5, 4)), DMA((5, 4)), DMA((7, 3)), DMA((7, 3)), DMA((7,)), DMA((7,)),
         ],
         compiler_params=pltpu.CompilerParams(
             collective_id=0, has_side_effects=True, vmem_limit_bytes=LIMIT
         ),
         name="layer",
-    )(text_rows[0], out_grad[0], image, meta, proj)
-
-    image_grad = image_out.reshape(NX, 2, SLOTS, HALF).transpose(2, 0, 1, 3).reshape(SLOTS, NX, HC)
-    image_grad = from_heads(image_grad)[None]
-    scale_grad = from_heads(sums[:, :10].reshape(NX, HC))
-    shift_grad = from_heads(sums[:, 10:20].reshape(NX, HC))
-    return (attn_out[None], text_grad[None], image_grad, scale_grad, shift_grad)
+    )(
+        text_rows[0], out_grad[0], image_rows[0], tile_counts, tile_offsets, doc_ids,
+        proj_scale.reshape(NX * HC // HD, HD), proj_shift.reshape(NX * HC // HD, HD),
+    )
+    results = (attn_out, text_grad, image_grad, scale_grad, shift_grad)
+    attn_out, text_grad, image_grad, scale_grad, shift_grad = pl.pallas_call(
+        land_kernel,
+        out_shape=tuple(shape(a.shape, a.dtype) for a in results),
+        in_specs=[VMEM] * 5,
+        out_specs=(ANY,) * 5,
+        scratch_shapes=[DMA((5,))],
+        name="land",
+    )(*results)
+    return (
+        attn_out[None], text_grad[None], image_grad[None],
+        scale_grad.reshape(NX * HC), shift_grad.reshape(NX * HC),
+    )
 
 
 def solution(mesh):

time: 144 us -> 126 us (0.88); the launches traced: 142 us -> 126 us
  local copies, waits for them, and re-layouts: 9.59 us -> 0 us
  other arithmetic: 4.47 us -> 0 us
  Pallas kernels: 126 us -> 123 us
    pallas_call x1, Pallas kernels: 126 us -> 120 us  [per_device(): pl.pallas_call(layer_kernel, out_shape=(shape((TOK, NX * QC), BF16), shap...]
    unnamed x11 -> x0, local copies, waits for them, and re-layouts: 4.23 us -> none
    slice x7 -> x0, local copies, waits for them, and re-layouts: 3.92 us -> none  [the longest x5 2.31 us: by_head(): a[..., :NX * QC].reshape(*lead, NX, QC)]
    pallas_call x0 -> x1, Pallas kernels: none -> 3.1 us  [per_device(): pl.pallas_call(land_kernel, out_shape=tuple((shape(a.shape, a.dtype) for...]
    concatenate x4 -> x0, other arithmetic: 2.5 us -> none  [the longest x2 1.23 us: from_heads(): return jnp.concatenate([part.reshape(*lead, -1) for part in parts], axis=-1)]
where the time goes in v3:
time: 126 us
  Pallas kernels  123 us (98%)
  between operations  2.09 us (2%)
    pallas_call x1, Pallas kernels, per_device(): pl.pallas_call(layer_kernel, out_shape=(shape((TOK, NX * QC), BF16), shap...  120 us
    pallas_call x1, Pallas kernels, per_device(): pl.pallas_call(land_kernel, out_shape=tuple((shape(a.shape, a.dtype) for...  3.1 us

profile of v3, /device:TPU:8, one launch (start us, length us, event | category | flops | bytes accessed | tf_op | source)
XLA Modules:
  0.0 125.5 jit_solution(13200219037015520026)
XLA Ops:
  1.9 120.3 %layer.1 = (bf16[128,4096]{1,0:T(8,128)(2,1)}, bf16[128,5120]{1,0:T(8,128)(2,1)}, bf16[8,5120]{1,0:T(8,128)(2,1)}, f32[40,128]{1,0:T(8,128)}, f32[40,128]{1,0:T(8,128)}) custom-call(bf16[128,5120]{1,0:T(8,128)(2,1)} %bitcast.10, bf16[128,4096]{1,0:T(8,128)(2,1)} %bitcast.11, bf16[8,5120]{1,0:T(8,128)(2,1)} %bitcast.12, s32[1,1]{1,0:T(1,128)S(6)} %copy.13.counts, ...), custom_call_target="tpu_custom_call" | custom-call | tf_op jit(solution)/shard_map/layer/pallas_call | solution.py:638
  122.3 3.1 %land.1 = (bf16[128,4096]{1,0:T(8,128)(2,1)}, bf16[128,5120]{1,0:T(8,128)(2,1)}, bf16[8,5120]{1,0:T(8,128)(2,1)}, f32[40,128]{1,0:T(8,128)}, f32[40,128]{1,0:T(8,128)}) custom-call(bf16[128,4096]{1,0:T(8,128)(2,1)} %get-tuple-element.15.refs_0_, bf16[128,5120]{1,0:T(8,128)(2,1)} %get-tuple-element.16.refs_1_, bf16[8,5120]{1,0:T(8,128)(2,1)} %get-tuple-element.17.refs_2_, ...), custom_call_target="tpu_custom_call" | custom-call | tf_op jit(solution)/shard_map/land/pallas_call | solution.py:711

commit v4 on v3

--- a/solution.py
+++ b/solution.py
@@ -162,15 +162,7 @@
             image_step(down, 1, d, k).start()
     send_x(2)
     send_x(3)
-
-    @pl.when(z <= NZ - 2)
-    def _():
-        for d in range(NX):
-            for k in range(2):
-                key_step(d, k).start()
-
     send_x(4)
-    send_x(5)
 
     ups, downs = [None], [None]
     for k in range(1, 3):
@@ -223,15 +215,22 @@
                 downs[k][j].start()
 
     pass_images(1)
+
+    @pl.when(z <= NZ - 2)
+    def _():
+        for d in range(NX):
+            for k in range(2):
+                key_step(d, k).start()
+
+    pass_images(2)
     for j in range(NX):
         pass_keys(1, j)
-    pass_images(2)
-    for j in range(NX):
-        pass_keys(2, j)
     pass_images(3)
     for k in range(4):
         arrived_x(k)
     pass_images(4)
+    for j in range(NX):
+        pass_keys(2, j)
 
     scale = of_head(proj_scale, x)
     shift = of_head(proj_shift, x)
@@ -257,6 +256,7 @@
         return hit, jnp.max(hit, axis=1, keepdims=True)
 
     arrived_x(4)
+    send_x(5)
 
     def place_queries(a, _):
         hit, is_image = chosen(base + a * TOK, TOK)
@@ -294,45 +294,46 @@
     within = jnp.concatenate([within] * REP, axis=1)
 
     def forward(s, a, at, size, keep_prob, diagonal):
-        value = jnp.dot(ks[s, at : at + size, :], q_t[a], preferred_element_type=F32)
-        if diagonal:
-            key_at = at + lax.broadcasted_iota(jnp.int32, (size, 1), 0)
-            value = jnp.where(key_at <= a * TOK + within, value, -1e30)
-        old = top[a]
-        new = jnp.maximum(old, jnp.max(value, axis=0, keepdims=True))
-        top[a] = new
-        tops[s, a] = new
-        factor = jnp.exp2((old - new) * (SCALE * LOG2E))
-        prob = jnp.exp2((value - new) * (SCALE * LOG2E))
-        total[a] = total[a] * factor + jnp.sum(prob, axis=0, keepdims=True)
-        prob_b = prob.astype(BF16)
-        keep_prob(prob_b)
-        acc_t[a] = acc_t[a] * factor + jnp.dot(vts[s, :, at : at + size], prob_b, preferred_element_type=F32)
+        lanes = [slice(k * 2 * HD, (k + 1) * 2 * HD) for k in range(LANES // (2 * HD))]
+        values = [jnp.dot(ks[s, at : at + size, :], q_t[a, :, ln], preferred_element_type=F32) for ln in lanes]
+        for value, ln in zip(values, lanes):
+            if diagonal:
+                key_at = at + lax.broadcasted_iota(jnp.int32, (size, 1), 0)
+                value = jnp.where(key_at <= a * TOK + within[:, ln], value, -1e30)
+            old = top[a, :, ln]
+            new = jnp.maximum(old, jnp.max(value, axis=0, keepdims=True))
+            top[a, :, ln] = new
+            tops[s, a, :, ln] = new
+            factor = jnp.exp2((old - new) * (SCALE * LOG2E))
+            prob = jnp.exp2((value - new) * (SCALE * LOG2E))
+            total[a, :, ln] = total[a, :, ln] * factor + jnp.sum(prob, axis=0, keepdims=True)
+            prob_b = prob.astype(BF16)
+            keep_prob(prob_b, ln)
+            acc_t[a, :, ln] = acc_t[a, :, ln] * factor + jnp.dot(
+                vts[s, :, at : at + size], prob_b, preferred_element_type=F32
+            )
 
     place_keys(WIN - 1, 0, ROW)
 
-    def forward_own(a, _):
+    for a in range(NX):
         pass_keys(3, a)
 
-        def keep_prob(prob):
-            p_buf[WIN - 2, a] = prob
-
-        forward(WIN - 1, a, 0, ROW, keep_prob, True)
-        return 0
-
-    lax.fori_loop(0, NX, forward_own, 0)
+        def keep_own(prob, ln):
+            p_buf[WIN - 2, a, : (a + 1) * TOK, ln] = prob
+
+        forward(WIN - 1, a, 0, (a + 1) * TOK, keep_own, True)
 
     def forward_row(k, _):
         s = WIN - 1 - k
         place_keys(s, 0, ROW)
 
         def one(a, _):
-            @pl.when(k == 1)
+            @pl.when(k == 2)
             def _():
                 pass_keys(4, a)
 
-            def keep_prob(prob):
-                p_buf[s - 1, a] = prob
+            def keep_prob(prob, ln):
+                p_buf[s - 1, a, :, ln] = prob
 
             forward(s, a, 0, ROW, keep_prob, False)
             return 0
@@ -347,8 +348,8 @@
         hop(4, NX - 1).wait_recv()
         place_keys(0, ROW - TOK, TOK)
 
-        def keep_prob(prob):
-            p_first[...] = prob
+        def keep_prob(prob, ln):
+            p_first[:, ln] = prob
 
         forward(0, 0, ROW - TOK, TOK, keep_prob, False)
 
@@ -408,27 +409,19 @@
         first_out[:, HD:] = dv.astype(BF16)
         first.start()
 
-    def backward_tile(s, a, begin):
-        dk, dv = backward(s, a, 0, ROW, p_buf[s - 1, a])
-
-        @pl.when(begin)
-        def _():
-            dkv[:, :HD] = dk
-            dkv[:, HD:] = dv
-
-        @pl.when(jnp.logical_not(begin))
-        def _():
-            dkv[:, :HD] += dk
-            dkv[:, HD:] += dv
+    def backward_tile(s, a, size):
+        dk, dv = backward(s, a, 0, size, p_buf[s - 1, a, :size, :])
+        dkv[s % 2, :size, :HD] += dk
+        dkv[s % 2, :size, HD:] += dv
 
     def summed(s, j):
         part = rows_of(j * TOK, TOK)
-        whole[part, :HD] = (dkv[part, :HD] * SCALE).astype(BF16)
-        whole[part, HD:] = dkv[part, HD:].astype(BF16)
+        whole[part, :HD] = (dkv[s % 2, part, :HD] * SCALE).astype(BF16)
+        whole[part, HD:] = dkv[s % 2, part, HD:].astype(BF16)
 
         def add(arrived):
-            whole[part, :HD] = (dkv[part, :HD] * SCALE + arrived[:, :HD].astype(F32)).astype(BF16)
-            whole[part, HD:] = (dkv[part, HD:] + arrived[:, HD:].astype(F32)).astype(BF16)
+            whole[part, :HD] = (dkv[s % 2, part, :HD] * SCALE + arrived[:, :HD].astype(F32)).astype(BF16)
+            whole[part, HD:] = (dkv[s % 2, part, HD:] + arrived[:, HD:].astype(F32)).astype(BF16)
 
         @pl.when((z <= NZ - 2) & ((s >= 2) | (j == NX - 1)))
         def _():
@@ -441,23 +434,39 @@
 
         return part
 
+    def pass_sums(s, j):
+        part = summed(s, j)
+        ring_out[s - 1, part, :] = whole[part, :]
+        ring(s - 1, j).start()
+
     for s in range(1, WIN - 1):
 
         @pl.when(z >= WIN - 1 - s)
         def _():
+            dkv[s % 2] = jnp.zeros((ROW, 2 * HD), F32)
+
             def one(a, _):
-                backward_tile(s, a, a == 0)
+                backward_tile(s, a, ROW)
+                if s >= 2:
+
+                    @pl.when(z >= WIN - s)
+                    def _():
+                        pass_sums(s - 1, a)
+
                 return 0
 
             lax.fori_loop(0, NX, one, 0)
-            for j in range(NX):
-                part = summed(s, j)
-                ring_out[s - 1, part, :] = whole[part, :]
-                ring(s - 1, j).start()
+
+    dkv[(WIN - 1) % 2] = jnp.zeros((ROW, 2 * HD), F32)
 
     def end(i, _):
         a = (x + i + 1) % NX
-        backward_tile(WIN - 1, a, i == 0)
+        for c in range(NX):
+
+            @pl.when(a == c)
+            def _():
+                backward_tile(WIN - 1, c, (c + 1) * TOK)
+
         kept = keep[rows_of(a * TOK, TOK), :]
         value = acc_t[a] * SCALE
         for r in range(REP):
@@ -465,6 +474,11 @@
             q_s[a, r * HD : (r + 1) * HD, :] = piece
             dq[a, :, r * HD : (r + 1) * HD] = (piece.astype(F32) * kept).astype(BF16)
         send_turn(i, 7, dq, text_grad.at[:, cols(x * QC, QC)])
+
+        @pl.when(z >= 1)
+        def _():
+            pass_sums(WIN - 2, i)
+
         return 0
 
     lax.fori_loop(0, NX, end, 0)
@@ -486,7 +500,7 @@
         ])
 
     def send_z(k):
-        for d in range(NZ - 1):
+        for d in (3, 2, 4, 1, 5, 0, 6):
             sent_z[d][k].start()
         own_z[k].start()
 
@@ -674,7 +688,7 @@
             pltpu.VMEM((NX, 1, LANES), F32),
             pltpu.VMEM((WIN, NX, 1, LANES), F32),
             pltpu.VMEM((NX, 1, LANES), F32),
-            pltpu.VMEM((ROW, 2 * HD), F32),
+            pltpu.VMEM((2, ROW, 2 * HD), F32),
             pltpu.VMEM((NX, TOK, QC), BF16),
             pltpu.VMEM((NX, TOK, QC), BF16),
             pltpu.VMEM((TOK, 2 * HD), BF16),

time: 126 us -> 120 us (0.952)
  Pallas kernels: 123 us -> 117 us
    pallas_call x1, Pallas kernels: 120 us -> 114 us  [per_device(): pl.pallas_call(layer_kernel, out_shape=(shape((TOK, NX * QC), BF16), shap...]
where the time goes in v4:
time: 120 us; the launch traced here: 119 us
  Pallas kernels  117 us (98%)
  between operations  2.09 us (2%)
    pallas_call x1, Pallas kernels, per_device(): pl.pallas_call(layer_kernel, out_shape=(shape((TOK, NX * QC), BF16), shap...  114 us
    pallas_call x1, Pallas kernels, per_device(): pl.pallas_call(land_kernel, out_shape=tuple((shape(a.shape, a.dtype) for...  3.1 us

profile of v4, /device:TPU:8, one launch (start us, length us, event | category | flops | bytes accessed | tf_op | source)
XLA Modules:
  0.0 118.7 jit_solution(5454211818546577884)
XLA Ops:
  1.9 113.5 %layer.1 = (bf16[128,4096]{1,0:T(8,128)(2,1)}, bf16[128,5120]{1,0:T(8,128)(2,1)}, bf16[8,5120]{1,0:T(8,128)(2,1)}, f32[40,128]{1,0:T(8,128)}, f32[40,128]{1,0:T(8,128)}) custom-call(bf16[128,5120]{1,0:T(8,128)(2,1)} %bitcast.10, bf16[128,4096]{1,0:T(8,128)(2,1)} %bitcast.11, bf16[8,5120]{1,0:T(8,128)(2,1)} %bitcast.12, s32[1,1]{1,0:T(1,128)S(6)} %copy.13.counts, ...), custom_call_target="tpu_custom_call" | custom-call | tf_op jit(solution)/shard_map/layer/pallas_call | solution.py:652
  115.5 3.1 %land.1 = (bf16[128,4096]{1,0:T(8,128)(2,1)}, bf16[128,5120]{1,0:T(8,128)(2,1)}, bf16[8,5120]{1,0:T(8,128)(2,1)}, f32[40,128]{1,0:T(8,128)}, f32[40,128]{1,0:T(8,128)}) custom-call(bf16[128,4096]{1,0:T(8,128)(2,1)} %get-tuple-element.15.refs_0_, bf16[128,5120]{1,0:T(8,128)(2,1)} %get-tuple-element.16.refs_1_, bf16[8,5120]{1,0:T(8,128)(2,1)} %get-tuple-element.17.refs_2_, ...), custom_call_target="tpu_custom_call" | custom-call | tf_op jit(solution)/shard_map/land/pallas_call | solution.py:725

commit v5 on v4

--- a/solution.py
+++ b/solution.py
@@ -228,9 +228,9 @@
     pass_images(3)
     for k in range(4):
         arrived_x(k)
-    pass_images(4)
     for j in range(NX):
         pass_keys(2, j)
+    pass_images(4)
 
     scale = of_head(proj_scale, x)
     shift = of_head(proj_shift, x)

time: 120 us -> 120 us (level)
  no operation moved by 1% of the time
where the time goes in v5:
time: 120 us; the launch traced here: 119 us
  Pallas kernels  116 us (97%)
  between operations  2.09 us (2%)
    pallas_call x1, Pallas kernels, per_device(): pl.pallas_call(layer_kernel, out_shape=(shape((TOK, NX * QC), BF16), shap...  113 us
    pallas_call x1, Pallas kernels, per_device(): pl.pallas_call(land_kernel, out_shape=tuple((shape(a.shape, a.dtype) for...  3.1 us

profile of v5, /device:TPU:8, one launch (start us, length us, event | category | flops | bytes accessed | tf_op | source)
XLA Modules:
  0.0 118.6 jit_solution(6546505609592821825)
XLA Ops:
  1.9 113.4 %layer.1 = (bf16[128,4096]{1,0:T(8,128)(2,1)}, bf16[128,5120]{1,0:T(8,128)(2,1)}, bf16[8,5120]{1,0:T(8,128)(2,1)}, f32[40,128]{1,0:T(8,128)}, f32[40,128]{1,0:T(8,128)}) custom-call(bf16[128,5120]{1,0:T(8,128)(2,1)} %bitcast.10, bf16[128,4096]{1,0:T(8,128)(2,1)} %bitcast.11, bf16[8,5120]{1,0:T(8,128)(2,1)} %bitcast.12, s32[1,1]{1,0:T(1,128)S(6)} %copy.13.counts, ...), custom_call_target="tpu_custom_call" | custom-call | tf_op jit(solution)/shard_map/layer/pallas_call | solution.py:652
  115.3 3.1 %land.1 = (bf16[128,4096]{1,0:T(8,128)(2,1)}, bf16[128,5120]{1,0:T(8,128)(2,1)}, bf16[8,5120]{1,0:T(8,128)(2,1)}, f32[40,128]{1,0:T(8,128)}, f32[40,128]{1,0:T(8,128)}) custom-call(bf16[128,4096]{1,0:T(8,128)(2,1)} %get-tuple-element.15.refs_0_, bf16[128,5120]{1,0:T(8,128)(2,1)} %get-tuple-element.16.refs_1_, bf16[8,5120]{1,0:T(8,128)(2,1)} %get-tuple-element.17.refs_2_, ...), custom_call_target="tpu_custom_call" | custom-call | tf_op jit(solution)/shard_map/land/pallas_call | solution.py:725
